TPU v7x, 512 devices: a whole 4x8x8 slice. The times are simulated.
512 devices in a mesh: expert: 64 (over y, z), head: 8 (over x, core).
Axes of the slice: x: 4, y: 8, z: 8, core: 2. Of those that a mesh axis runs over, the one named last changes fastest.
Arguments:
- queries: bfloat16 [2, 2048, 2048], P(None, 'expert', 'head'), may hold values from -12 to 12
- cache_band: bfloat16 [2048, 128, 1024], P('expert', None, 'head'), may hold values from -12 to 12
- new_kv: bfloat16 [2, 2048, 1024], P(None, 'expert', 'head'), may hold values from -4 to 4
- cache_lengths: int32 [2048], P('expert'), may hold values from 1 to 8192
- sink_logits: float32 [32], P('head'), may hold values from -6 to 6
- o_weight: bfloat16 [2048, 2880], P('head'), may hold values from -0.75 to 0.75
- residual: bfloat16 [2, 2048, 2880], P(None, 'expert', 'head'), may hold values from -54 to 54
- norm_gain: float32 [2880], replicated, may hold values from 0.1 to 1.9
- route_logits: float32 [2, 2048, 4], P(None, 'expert'), may hold values from -8 to 400
- routes: int32 [2, 2048, 4], P(None, 'expert'), may hold values from 0 to 31, as said below
- old_experts: int32 [32], replicated, may hold values from 0 to 31, each once
- new_experts: int32 [32], replicated, may hold values from 0 to 31, each once
- train_gate_up: bfloat16 [32, 2880, 2, 2048], P(None, 'expert', None, 'head'), may hold values from -0.21875 to 0.21875
- train_down: bfloat16 [32, 2880, 2048], P(None, 'expert', 'head'), may hold values from -0.125 to 0.125
Outputs:
- layer_out: bfloat16 [2, 2048, 2880], P(None, 'expert', 'head')
- synced_down: bfloat16 [64, 2880, 1024], P('expert', None, 'head')
Inputs may be any that keep to these rules, and one draw needn't show every extreme that they name: `old_experts`: a permutation. `new_experts`: a permutation. `routes`: each row names 4 different experts; in each step and each aligned block of 32 sequences (one device's rows) no expert is named by more than 8 rows, and in each step one expert is named by exactly 8 rows of every block.
All inputs are finite; a program needn't handle non-finite values.
Results may differ from a plain program's by a relative error of at most 0.028.
Values may be sent and summed in bfloat16 or wider, within the bound.
A program may use at most 128 MiB of HBM per device.

v0:
```python
import jax
import jax.numpy as jnp
from jax import lax
from jax.sharding import PartitionSpec as P

D = 2880
HD = 64
TOP = 4
STEPS = 2


EPSILON = 1e-05


def attend(step_index, queries, extended, cache_lengths, sink_logits):
    seq_count = queries.shape[1]
    query_width = queries.shape[2]
    window_size = extended.shape[1] - 2
    kv_local = extended.shape[2] // (2 * HD)
    group_size = query_width // (kv_local * HD)
    query_rows = queries[step_index].reshape(seq_count, kv_local, group_size, HD)
    visible_slots = lax.slice_in_dim(extended, step_index + 1, step_index + 1 + window_size, axis=1)
    visible_slots = visible_slots.reshape(seq_count, window_size, kv_local, 2, HD)
    key_rows = visible_slots[:, :, :, 0, :]
    value_rows = visible_slots[:, :, :, 1, :]
    scores = jnp.einsum(
        "svgd,swvd->svgw", query_rows, key_rows, preferred_element_type=jnp.float32
    ) * HD ** (-0.5)
    slot_index = step_index + 1 + jnp.arange(window_size, dtype=jnp.int32)
    visible = slot_index[None, :] >= (window_size - cache_lengths)[:, None]
    scores = jnp.where(visible[:, None, None, :], scores, -1e30)
    sink_part = sink_logits.reshape(kv_local, group_size)[None, :, :, None]
    row_top = jnp.maximum(jnp.max(scores, axis=-1, keepdims=True), sink_part)
    raised = jnp.exp(scores - row_top)
    sum_raised = jnp.sum(raised, axis=-1, keepdims=True) + jnp.exp(sink_part - row_top)
    probabilities = (raised / sum_raised).astype(jnp.bfloat16)
    mixed_values = jnp.einsum(
        "svgw,swvd->svgd", probabilities, value_rows, preferred_element_type=jnp.float32
    )
    return mixed_values.astype(jnp.bfloat16).reshape(seq_count, query_width)


def local(
    queries,
    cache_band,
    new_kv,
    cache_lengths,
    sink_logits,
    o_weight,
    residual,
    norm_gain,
    route_logits,
    routes,
    old_experts,
    new_experts,
    train_gate_up,
    train_down,
):
    expert_count = old_experts.shape[0]
    device_count = lax.axis_size("expert")
    parity = lax.axis_index("expert") % 2
    head_index = lax.axis_index("head")
    local_ff = train_gate_up.shape[3]
    half_ff = local_ff // 2
    seq_count = queries.shape[1]
    share_width = residual.shape[2]
    share_start = head_index * share_width
    counter = jnp.arange(expert_count, dtype=jnp.int32)
    train_pos = jnp.sum(
        jnp.where(old_experts[None, :] == new_experts[:, None], counter[None, :], 0), axis=1
    )
    slot_of = jnp.sum(
        jnp.where(new_experts[None, :] == counter[:, None], counter[None, :], 0), axis=1
    )
    dest_pos = jnp.repeat(train_pos, 2, total_repeat_length=device_count)
    stacked = jnp.concatenate(
        [train_gate_up[dest_pos], train_down[dest_pos][:, :, None, :]], axis=2
    )
    moved_weights = lax.all_to_all(stacked, "expert", split_axis=0, concat_axis=1, tiled=True)[0]
    weight_in = moved_weights[:, :2, :]
    weight_down = moved_weights[:, 2, :]
    synced_down = lax.dynamic_slice_in_dim(weight_down, parity * half_ff, half_ff, 1)[None]
    capacity_half = 2 * seq_count * TOP // expert_count // 2
    slot_rows = device_count * capacity_half
    extended = jnp.concatenate([cache_band, jnp.swapaxes(new_kv, 0, 1)], axis=1)
    outputs = []
    for step_index in range(STEPS):
        attended = attend(step_index, queries, extended, cache_lengths, sink_logits)
        partial_value = jnp.dot(attended, o_weight, preferred_element_type=jnp.float32)
        own_block = lax.dynamic_slice_in_dim(partial_value, share_start, share_width, 1) + residual[
            step_index
        ].astype(jnp.float32)
        placed = lax.dynamic_update_slice_in_dim(partial_value, own_block, share_start, 1)
        hidden = lax.psum(placed.astype(jnp.bfloat16), "head").astype(jnp.float32)
        mean_square = jnp.mean(hidden * hidden, axis=1, keepdims=True)
        normed = (hidden * lax.rsqrt(mean_square + EPSILON) * norm_gain).astype(jnp.bfloat16)
        own_share = lax.dynamic_slice_in_dim(hidden, share_start, share_width, 1)
        route_weight = jax.nn.softmax(route_logits[step_index], axis=-1)
        flat_routes = routes[step_index].reshape(-1)
        entry_index = jnp.arange(flat_routes.shape[0], dtype=jnp.int32)
        earlier = (flat_routes[:, None] == flat_routes[None, :]) & (
            entry_index[None, :] < entry_index[:, None]
        )
        route_rank = jnp.sum(earlier.astype(jnp.int32), axis=1)
        destination = (
            (2 * slot_of[flat_routes] + route_rank % 2) * capacity_half + route_rank // 2
        ).reshape(seq_count, TOP)
        slot_index = jnp.arange(slot_rows, dtype=jnp.int32)
        placing = jnp.any(slot_index[:, None, None] == destination[None], axis=2).astype(
            jnp.bfloat16
        )
        outgoing = jnp.dot(placing, normed, preferred_element_type=jnp.float32).astype(jnp.bfloat16)
        outgoing = outgoing.reshape(device_count, capacity_half, D)
        arrived = lax.all_to_all(outgoing, "expert", split_axis=0, concat_axis=0, tiled=True)
        block_rows = arrived.shape[1]
        token_rows = arrived.reshape(-1, arrived.shape[2])
        projected = jnp.einsum(
            "rd,dcf->rcf", token_rows, weight_in, preferred_element_type=jnp.float32
        )
        gate_value = jnp.minimum(projected[:, 0], 7.0)
        up_value = jnp.clip(projected[:, 1], -7.0, 7.0)
        active = ((up_value + 1.0) * gate_value * jax.nn.sigmoid(1.702 * gate_value)).astype(
            jnp.bfloat16
        )
        partial_out = lax.dot_general(
            active, weight_down, (((1,), (1,)), ((), ())), preferred_element_type=jnp.float32
        ).astype(jnp.bfloat16)
        summed = lax.psum_scatter(
            partial_out.astype(jnp.float32).astype(jnp.bfloat16),
            "head",
            scatter_dimension=1,
            tiled=True,
        ).astype(jnp.float32)
        returned = lax.all_to_all(
            summed.reshape(device_count, block_rows, -1).astype(jnp.bfloat16),
            "expert",
            split_axis=0,
            concat_axis=0,
            tiled=True,
        ).astype(jnp.float32)
        returned = returned.reshape(slot_rows, -1)
        combining = jnp.sum(
            jnp.where(
                destination[:, :, None] == slot_index[None, None, :], route_weight[:, :, None], 0.0
            ),
            axis=1,
        )
        expert_mix = jnp.dot(combining, returned, precision=lax.Precision.HIGHEST)
        outputs.append((own_share + expert_mix).astype(jnp.bfloat16))
    return (jnp.stack(outputs), synced_down)


def solution(mesh):
    in_specs = (
        P(None, "expert", "head"),
        P("expert", None, "head"),
        P(None, "expert", "head"),
        P("expert"),
        P("head"),
        P("head", None),
        P(None, "expert", "head"),
        P(),
        P(None, "expert", None),
        P(None, "expert", None),
        P(),
        P(),
        P(None, "expert", None, "head"),
        P(None, "expert", "head"),
    )
    out_specs = (P(None, "expert", "head"), P("expert", None, "head"))
    return jax.shard_map(local, mesh=mesh, in_specs=in_specs, out_specs=out_specs, check_vma=False)
```

profile of v0, /device:TPU:56, one launch (start us, length us, event | category | flops | bytes accessed | tf_op | source)
XLA Modules:
  0.0 462.6 jit_solution(4108536874031952936)
XLA Ops:
  7.3 1.7 copy.108
  10.6 2.9 fusion.16
  16.2 1.5 convolution_convert_fusion.5
  20.6 1.5 dynamic_update_slice.7
  22.1 1.7 convert_element_type.118
  27.4 73.1 %all-reduce.3.cloned.1.call-done = (bf16[32,2880]{1,0:T(8,128)(2,1)}, bf16[32,2880]{1,0:T(8,128)(2,1)}) async-done(((bf16[32,2880]{1,0:T(8,128)(2,1)}, bf16[32,2880]{1,0:T(8,128)(2,1)}), (bf16[32,2880]{1,0:T(8,128)(2,1)}, bf16[32,2880]{1,0:T(8,128)(2,1)})) %all-reduce.3.cloned.1.call-update) | async-done | bytes 368656 | tf_op jit(solution)/shard_map/psum | solution.py:94
  101.6 2.7 convolution_convert_fusion
  104.3 1.8 copy.127
  107.5 14.4 %all-to-all-start.3 = ((bf16[64,4,2880]{2,1,0:T(4,128)(2,1)}), bf16[64,4,2880]{2,1,0:T(4,128)(2,1)}, u32[]{:S(2)}, u32[]{:S(2)}) async-start(bf16[64,4,2880]{2,1,0:T(4,128)(2,1)} %reshape.705), calls=%async_computation.4 | async-start | bytes 3014656 | tf_op jit(solution)/shard_map/all_to_all | solution.py:114
  122.7 5.9 %gather_fusion.3 = bf16[64,45,256]{2,0,1:T(8,128)(2,1)} fusion(bf16[32,45,256]{2,0,1:T(8,128)(2,1)S(1)} %copy-done.2, s32[1024]{0:T(1024)S(1)} %pad_clamp_fusion.1), kind=kCustom, calls=%fused_computation.3 | custom fusion | bytes 2949376 | tf_op jit(solution)/shard_map/gather | solution.py:77
  128.7 5.2 %copy.116 = bf16[64,45,1,256]{3,2,1,0:T(2,128)(2,1)} copy(bf16[64,45,1,256]{3,0,2,1:T(8,128)(2,1)} %bitcast.99) | data formatting | bytes 2949120 | tf_op jit(solution)/shard_map/broadcast_in_dim | solution.py:77
  133.9 8.8 %gather_fusion.2 = bf16[64,45,2,256]{3,2,1,0:T(2,128)(2,1)} fusion(bf16[32,45,2,256]{3,2,1,0:T(2,128)(2,1)S(1)} %copy-done, s32[1024]{0:T(1024)S(1)} %pad_clamp_fusion.1), kind=kCustom, calls=%fused_computation.2 | custom fusion | bytes 5898496 | tf_op jit(solution)/shard_map/gather | solution.py:77
  142.7 8.8 %pad_maximum_fusion = bf16[64,45,3,256]{3,2,1,0:T(4,128)(2,1)S(1)} fusion(bf16[64,45,1,256]{3,2,1,0:T(2,128)(2,1)} %copy.116, bf16[64,45,2,256]{3,2,1,0:T(2,128)(2,1)} %gather_fusion.2), kind=kLoop, calls=%fused_computation.5 | loop fusion | flops 8847360 | bytes 8847360 | tf_op jit(solution)/shard_map/concatenate | solution.py:76
  151.5 3.2 copy.117
  154.7 2.7 all-to-all-done.3
  157.4 10.3 %all-to-all-start.1 = ((bf16[64,45,3,256]{3,1,2,0:T(8,128)(2,1)}), bf16[64,45,3,256]{3,1,2,0:T(8,128)(2,1)}, u32[]{:S(2)}, u32[]{:S(2)}) async-start(bf16[64,45,3,256]{3,1,2,0:T(8,128)(2,1)} %copy.117), calls=%async_computation.1 | async-start | bytes 9437184 | tf_op jit(solution)/shard_map/all_to_all | solution.py:79
  173.0 3.6 reshape.706
  176.6 117.7 %all-to-all-done.1 = bf16[64,45,3,256]{3,1,2,0:T(8,128)(2,1)} async-done(((bf16[64,45,3,256]{3,1,2,0:T(8,128)(2,1)}), bf16[64,45,3,256]{3,1,2,0:T(8,128)(2,1)}, u32[]{:S(2)}, u32[]{:S(2)}) %all-to-all-start.1) | async-done | bytes 4423712 | tf_op jit(solution)/shard_map/all_to_all | solution.py:79
  294.4 26.1 %all-to-all-start = ((bf16[64,4,2880]{2,1,0:T(4,128)(2,1)}), bf16[64,4,2880]{2,1,0:T(4,128)(2,1)S(1)}, u32[]{:S(2)}, u32[]{:S(2)}) async-start(bf16[64,4,2880]{2,1,0:T(4,128)(2,1)} %reshape.697), calls=%async_computation | async-start | bytes 3014656 | tf_op jit(solution)/shard_map/all_to_all | solution.py:114
  320.7 5.0 %copy.118 = bf16[64,45,3,256]{3,1,0,2:T(8,128)(2,1)} copy(bf16[64,45,3,256]{3,1,2,0:T(8,128)(2,1)} %all-to-all-done.1) | data formatting | bytes 8847360 | tf_op jit(solution)/shard_map/all_to_all | solution.py:79
  325.7 7.3 %squeeze.9 = bf16[2880,3,256]{2,0,1:T(8,128)(2,1)} reshape(bf16[64,45,3,256]{3,1,0,2:T(8,128)(2,1)} %copy.118) | data formatting | bytes 8847360 | tf_op jit(solution)/shard_map/squeeze | solution.py:79
  333.0 3.4 fusion
  336.6 1.8 convolution_convert_fusion.2
  338.5 18.3 %all-to-all-done = bf16[64,4,2880]{2,1,0:T(4,128)(2,1)S(1)} async-done(((bf16[64,4,2880]{2,1,0:T(4,128)(2,1)}), bf16[64,4,2880]{2,1,0:T(4,128)(2,1)S(1)}, u32[]{:S(2)}, u32[]{:S(2)}) %all-to-all-start) | async-done | bytes 1474592 | tf_op jit(solution)/shard_map/all_to_all | solution.py:114
  356.7 1.6 reshape.698
  358.4 3.3 fusion.2
  361.6 3.1 convolution_convert_fusion.3
  364.8 23.7 %reduce-scatter.5.cloned.1.call-done = bf16[256,360]{0,1:T(8,128)(2,1)} async-done(((bf16[256,2880]{0,1:T(8,128)(2,1)}), bf16[256,360]{0,1:T(8,128)(2,1)}) %reduce-scatter.5.cloned.1.call-update) | async-done | bytes 184336 | tf_op jit(solution)/shard_map/reduce_scatter | solution.py:128
  390.3 13.5 %all-to-all-start.4 = ((bf16[64,4,360]{2,1,0:T(4,128)(2,1)}), bf16[64,4,360]{2,1,0:T(4,128)(2,1)S(1)}, u32[]{:S(2)}, u32[]{:S(2)}) async-start(bf16[64,4,360]{2,1,0:T(4,128)(2,1)} %convert_element_type.126), calls=%async_computation.6 | async-start | bytes 393216 | tf_op jit(solution)/shard_map/all_to_all | solution.py:134
  405.7 22.9 %reduce-scatter.3.cloned.1.call-done = bf16[256,360]{0,1:T(8,128)(2,1)} async-done(((bf16[256,2880]{0,1:T(8,128)(2,1)}), bf16[256,360]{0,1:T(8,128)(2,1)}) %reduce-scatter.3.cloned.1.call-update) | async-done | bytes 184336 | tf_op jit(solution)/shard_map/reduce_scatter | solution.py:128
  430.4 13.3 %all-to-all-start.2 = ((bf16[64,4,360]{2,1,0:T(4,128)(2,1)}), bf16[64,4,360]{2,1,0:T(4,128)(2,1)S(1)}, u32[]{:S(2)}, u32[]{:S(2)}) async-start(bf16[64,4,360]{2,1,0:T(4,128)(2,1)} %convert_element_type.112), calls=%async_computation.3 | async-start | bytes 393216 | tf_op jit(solution)/shard_map/all_to_all | solution.py:134
  445.9 8.2 %all-to-all-done.2 = bf16[64,4,360]{2,1,0:T(4,128)(2,1)S(1)} async-done(((bf16[64,4,360]{2,1,0:T(4,128)(2,1)}), bf16[64,4,360]{2,1,0:T(4,128)(2,1)S(1)}, u32[]{:S(2)}, u32[]{:S(2)}) %all-to-all-start.2) | async-done | bytes 184352 | tf_op jit(solution)/shard_map/all_to_all | solution.py:134
  (125 shorter events, 28.9 us)
Async XLA Ops:
  7.2 126.7 %copy-start = (bf16[32,45,2,256]{3,2,1,0:T(2,128)(2,1)S(1)}, bf16[32,45,2,256]{3,2,1,0:T(2,128)(2,1)}, u32[]{:S(2)}) copy-start(bf16[32,45,2,256]{3,2,1,0:T(2,128)(2,1)} %param.28) | copy-start | bytes 4423684
  7.2 1.8 copy-start.12
  7.2 3.2 copy-start.11
  7.2 3.3 copy-start.18
  7.2 93.3 %all-reduce.3.cloned.1.call-start = ((), (), s32[]{:S(2)}) async-start(), calls=%async_computation.9 | async-start | bytes 753664 | tf_op jit(solution)/shard_map/psum | solution.py:94
  10.6 4.2 copy-start.13
  13.5 1.0 copy-start.7
  14.5 3.2 copy-start.4
  17.6 2.0 copy-start.9
  19.0 6.0 %copy-start.14 = (s32[2,32,4]{1,2,0:T(4,128)S(1)}, s32[2,32,4]{1,2,0:T(4,128)}, u32[]{:S(2)}) copy-start(s32[2,32,4]{1,2,0:T(4,128)} %param.25) | copy-start | bytes 3076
  19.0 6.3 %copy-start.15 = (s32[32]{0:T(128)S(1)}, s32[32]{0:T(128)}, u32[]{:S(2)}) copy-start(s32[32]{0:T(128)} %param.27) | copy-start | bytes 388
  19.0 6.3 %copy-start.16 = (s32[32]{0:T(128)S(1)}, s32[32]{0:T(128)}, u32[]{:S(2)}) copy-start(s32[32]{0:T(128)} %param.26) | copy-start | bytes 388
  19.1 82.5 %copy-start.8 = (f32[2880]{0:T(1024)S(1)}, f32[2880]{0:T(1024)}, u32[]{:S(2)}) copy-start(f32[2880]{0:T(1024)} %param.23) | copy-start | bytes 34564
  107.4 14.5 %copy-start.17 = (s32[64]{0:T(128)S(1)}, s32[64]{0:T(128)}, u32[]{:S(2)}) copy-start(s32[64]{0:T(128)} %constant.188) | copy-start | bytes 772
  107.5 15.3 %copy-start.2 = (bf16[32,45,256]{2,0,1:T(8,128)(2,1)S(1)}, bf16[32,45,256]{2,0,1:T(8,128)(2,1)}, u32[]{:S(2)}) copy-start(bf16[32,45,256]{2,0,1:T(8,128)(2,1)} %param.29) | copy-start | bytes 2211844
  107.5 49.9 %all-to-all-start.3 = ((bf16[64,4,2880]{2,1,0:T(4,128)(2,1)}), bf16[64,4,2880]{2,1,0:T(4,128)(2,1)}, u32[]{:S(2)}, u32[]{:S(2)}) async-start(bf16[64,4,2880]{2,1,0:T(4,128)(2,1)} %reshape.705), calls=%async_computation.4 | async-start | bytes 3014656 | tf_op jit(solution)/shard_map/all_to_all | solution.py:114
  154.7 15.2 %copy-start.5 = (bf16[32,2880]{1,0:T(8,128)(2,1)S(1)}, bf16[32,2880]{1,0:T(8,128)(2,1)}, u32[]{:S(2)}) copy-start(bf16[32,2880]{1,0:T(8,128)(2,1)} %get-tuple-element.21) | copy-start | bytes 552964
  157.4 137.0 %all-to-all-start.1 = ((bf16[64,45,3,256]{3,1,2,0:T(8,128)(2,1)}), bf16[64,45,3,256]{3,1,2,0:T(8,128)(2,1)}, u32[]{:S(2)}, u32[]{:S(2)}) async-start(bf16[64,45,3,256]{3,1,2,0:T(8,128)(2,1)} %copy.117), calls=%async_computation.1 | async-start | bytes 9437184 | tf_op jit(solution)/shard_map/all_to_all | solution.py:79
  294.4 62.4 %all-to-all-start = ((bf16[64,4,2880]{2,1,0:T(4,128)(2,1)}), bf16[64,4,2880]{2,1,0:T(4,128)(2,1)S(1)}, u32[]{:S(2)}, u32[]{:S(2)}) async-start(bf16[64,4,2880]{2,1,0:T(4,128)(2,1)} %reshape.697), calls=%async_computation | async-start | bytes 3014656 | tf_op jit(solution)/shard_map/all_to_all | solution.py:114
  320.5 68.0 %reduce-scatter.5.cloned.1.call-start = ((), (), s32[]{:S(2)}) async-start(), calls=%async_computation.8 | async-start | bytes 1658880 | tf_op jit(solution)/shard_map/reduce_scatter | solution.py:128
  333.0 3.6 copy-start.3
  338.4 90.2 %reduce-scatter.3.cloned.1.call-start = ((), (), s32[]{:S(2)}) async-start(), calls=%async_computation.7 | async-start | bytes 1658880 | tf_op jit(solution)/shard_map/reduce_scatter | solution.py:128
  361.6 3.2 copy-start.10
  364.8 39.3 %copy-start.6 = (bf16[32,2880]{1,0:T(8,128)(2,1)S(1)}, bf16[32,2880]{1,0:T(8,128)(2,1)}, u32[]{:S(2)}) copy-start(bf16[32,2880]{1,0:T(8,128)(2,1)} %get-tuple-element.20) | copy-start | bytes 552964
  390.3 40.1 %all-to-all-start.4 = ((bf16[64,4,360]{2,1,0:T(4,128)(2,1)}), bf16[64,4,360]{2,1,0:T(4,128)(2,1)S(1)}, u32[]{:S(2)}, u32[]{:S(2)}) async-start(bf16[64,4,360]{2,1,0:T(4,128)(2,1)} %convert_element_type.126), calls=%async_computation.6 | async-start | bytes 393216 | tf_op jit(solution)/shard_map/all_to_all | solution.py:134
  405.6 38.1 %slice-start = ((bf16[2880,3,256]{2,0,1:T(8,128)(2,1)}), bf16[2880,1,256]{2,0,1:T(8,128)(2,1)S(1)}, s32[]{:S(2)}) async-start(bf16[2880,3,256]{2,0,1:T(8,128)(2,1)} %squeeze.9), calls=%async_computation.10 | async-start | bytes 2949120 | tf_op jit(solution)/shard_map/slice | solution.py:81
  405.7 50.2 %copy-start.1 = (bf16[32,45,2,256]{3,2,1,0:T(2,128)(2,1)S(1)}, bf16[32,45,2,256]{3,2,1,0:T(2,128)(2,1)}, u32[]{:S(2)}) copy-start(bf16[32,45,2,256]{3,2,1,0:T(2,128)(2,1)} %param.28) | copy-start | bytes 4423684
  430.4 23.7 %all-to-all-start.2 = ((bf16[64,4,360]{2,1,0:T(4,128)(2,1)}), bf16[64,4,360]{2,1,0:T(4,128)(2,1)S(1)}, u32[]{:S(2)}, u32[]{:S(2)}) async-start(bf16[64,4,360]{2,1,0:T(4,128)(2,1)} %convert_element_type.112), calls=%async_computation.3 | async-start | bytes 393216 | tf_op jit(solution)/shard_map/all_to_all | solution.py:134
Sparse Core Ops, SparseCore 0:
  25.1 75.3 all-reduce.2
  338.5 49.9 reduce-scatter.4
  391.6 36.9 reduce-scatter.2
where the time goes:
time: 471 us; the launch traced here: 463 us
  waiting for transfers between devices  267 us (57%)
  starting transfers between devices  78.1 us (17%)
  local copies, waits for them, and re-layouts  61.9 us (13%)
  matrix products  21.5 us (5%)
  other arithmetic  19.9 us (4%)
  between operations  14.5 us (3%)
    all_to_all x1, waiting for transfers between devices, local(): lax.all_to_all(stacked, 'expert', split_axis=0, concat_axis=1, tiled=True)  118 us
    psum x1, waiting for transfers between devices, local(): hidden = lax.psum(placed.astype(jnp.bfloat16), 'head').astype(jnp.float32)  73.1 us
    reduce_scatter x2, waiting for transfers between devices, local(): lax.psum_scatter(partial_out.astype(jnp.float32).astype(jnp.bfloat16), 'h...  46.6 us
    all_to_all x2, starting transfers between devices, local(): lax.all_to_all(outgoing, 'expert', split_axis=0, concat_axis=0, tiled=True)  40.5 us
    all_to_all x2, starting transfers between devices, local(): lax.all_to_all(summed.reshape(device_count, block_rows, -1).astype(jnp.bf...  26.9 us
    all_to_all x2, waiting for transfers between devices, local(): lax.all_to_all(outgoing, 'expert', split_axis=0, concat_axis=0, tiled=True)  21 us
    all_to_all x1, starting transfers between devices, local(): lax.all_to_all(stacked, 'expert', split_axis=0, concat_axis=1, tiled=True)  10.3 us
  transfers between devices with their start and end apart: 8, of which 7 were waited for; matrix products, arithmetic and copies ran while one was open for 17% of the time, Pallas kernels for 0%

commit v1 on v0

v1 whole, which is shorter than its diff:
```python
import functools
import jax
import jax.numpy as jnp
from jax import lax
from jax.experimental import pallas as pl
from jax.experimental.pallas import tpu as pltpu
from jax.sharding import PartitionSpec as P

HD = 64
TOP = 4
STEPS = 2
GROUP = 4
CAP = 8
ROWS = STEPS * CAP
EPSILON = 1e-05
CHUNKS = 4
MESH = pl.DeviceIdType.MESH
BF = jnp.bfloat16
F32 = jnp.float32
EXACT = lax.Precision.HIGHEST


def iota(shape, dim):
    return lax.broadcasted_iota(jnp.int32, shape, dim)


def dot(a, b, dims=((1,), (0,)), precision=None):
    return lax.dot_general(a, b, (dims, ((), ())), preferred_element_type=F32, precision=precision)


def column(row, size):
    eye = iota((size, size), 0) == iota((size, size), 1)
    return jnp.sum(jnp.where(eye, row, 0.0), axis=1, keepdims=True)


def log2(n):
    assert n & (n - 1) == 0
    return n.bit_length() - 1


def kernel(
    n_expert,
    n_head,
    pos_ref,
    new_ref,
    len_ref,
    sink_ref,
    logit_ref,
    route_ref,
    gain_ref,
    query_ref,
    band_ref,
    new_kv_ref,
    o_ref,
    residual_ref,
    gate_up_ref,
    down_ref,
    out_ref,
    sync_ref,
    down_f,
    gu_out,
    dn_out,
    gu_in,
    dn_in,
    part_out,
    part_in,
    tok_out,
    tok_all,
    y_out,
    y_in,
    z_out,
    z_in,
    ret_out,
    ret_in,
    sync_f,
    sem,
    ag_sem,
    rs_sem,
):
    experts = n_expert // 2
    n_chip = n_head // 2
    seqs = query_ref.shape[1]
    cols = STEPS * seqs
    block = gate_up_ref.shape[1]
    padded = gu_in.shape[1]
    share = residual_ref.shape[2]
    per_head = n_expert // n_head
    wide = per_head * padded
    width = n_head * share
    half = gate_up_ref.shape[3] // 2
    seq_bits = log2(seqs)

    me = lax.axis_index("expert")
    head = lax.axis_index("head")
    core = lax.rem(head, 2)
    chip = head // 2
    mate = head + 1 - 2 * core
    my_slot = me // 2
    partner = me + 1 - 2 * lax.rem(me, 2)
    my_half = lax.rem(me, 2)

    barrier = pltpu.get_barrier_semaphore()

    def greet_expert(i, carry):
        pl.semaphore_signal(
            barrier, inc=1, device_id=(lax.rem(me + i, n_expert), head), device_id_type=MESH
        )
        return carry

    def greet_head(i, carry):
        pl.semaphore_signal(
            barrier, inc=1, device_id=(me, lax.rem(head + i, n_head)), device_id_type=MESH
        )
        return carry

    lax.fori_loop(1, n_expert, greet_expert, 0)
    lax.fori_loop(1, n_head, greet_head, 0)

    for p in range(2):
        down_f[p] = (
            down_ref[:, :, p * half : (p + 1) * half].astype(F32).reshape(block * experts, half)
        )
    pad = padded - block
    tail = padded - 16 if padded >= 16 else 0
    gu_out[:, :, tail:, :] = jnp.zeros((experts, 2, padded - tail, 2 * half), BF)
    dn_out[:, :, tail:, :] = jnp.zeros((experts, 2, padded - tail, half), BF)

    pl.semaphore_wait(barrier, n_expert + n_head - 2)

    GU_S, GU_R, DN_S, DN_R, PART_S, PART_R, TOK_S, TOK_R, RET_S, RET_R, AG_S, Y_S, Z_S = range(13)

    def send(src, dst, e, h, s, r):
        pltpu.make_async_remote_copy(
            src_ref=src,
            dst_ref=dst,
            send_sem=s,
            recv_sem=r,
            device_id=(e, h),
            device_id_type=MESH,
        ).start()

    def drain(ref, s):
        pltpu.make_async_copy(ref, ref, s).wait()

    def prepare_gate_up(slot):
        index = pos_ref[slot]
        for p in range(2):
            for c in range(2):
                gu_out[slot, p, :block, c * half : (c + 1) * half] = gate_up_ref[
                    index, :, c, p * half : (p + 1) * half
                ]

    def prepare_down(slot):
        index = pos_ref[slot]
        for p in range(2):
            dn_out[slot, p, :block, :] = down_f[
                p, pl.ds(index, block, stride=experts), :
            ].astype(BF)

    def send_gate_up(i, carry):
        slot = lax.rem(my_slot + i, experts)
        prepare_gate_up(slot)
        for p in range(2):
            send(gu_out.at[slot, p], gu_in.at[me], 2 * slot + p, head, sem.at[GU_S], sem.at[GU_R])
        return carry

    def send_down(i, carry):
        slot = lax.rem(my_slot + i, experts)
        prepare_down(slot)
        for p in range(2):
            send(dn_out.at[slot, p], dn_in.at[me], 2 * slot + p, head, sem.at[DN_S], sem.at[DN_R])
        return carry

    prepare_gate_up(my_slot)
    prepare_down(my_slot)
    send(gu_out.at[my_slot, 1 - my_half], gu_in.at[me], partner, head, sem.at[GU_S], sem.at[GU_R])
    send(dn_out.at[my_slot, 1 - my_half], dn_in.at[me], partner, head, sem.at[DN_S], sem.at[DN_R])
    gu_in[me] = gu_out[my_slot, my_half]
    dn_in[me] = dn_out[my_slot, my_half]
    first_batch = experts // 2
    lax.fori_loop(1, first_batch, send_gate_up, 0)

    lanes = 2 * HD
    rows = STEPS * GROUP * seqs
    r_id = iota((rows, cols), 0)
    c_id = iota((rows, cols), 1)
    same = ((r_id >> 3) == (c_id & (seqs - 1))) & (((r_id >> 2) & 1) == (c_id >> seq_bits))
    rt_id = iota((cols, rows), 1)
    ct_id = iota((cols, rows), 0)
    same_t = ((rt_id >> 3) == (ct_id & (seqs - 1))) & (((rt_id >> 2) & 1) == (ct_id >> seq_bits))
    flat_q = query_ref[...].reshape(cols, GROUP * HD)
    spread_q = jnp.zeros((rows, lanes), F32)
    for g in range(GROUP):
        k_id = iota((GROUP * HD, lanes), 0)
        l_id = iota((GROUP * HD, lanes), 1)
        pick = ((k_id == g * HD + l_id) & (l_id < HD)).astype(BF)
        part = dot(flat_q, pick).astype(BF)
        spread_q += dot((same & ((r_id & 3) == g)).astype(BF), part)
    repeat = ((iota((rows, seqs), 0) >> 3) == iota((rows, seqs), 1)).astype(BF)
    fresh = [dot(repeat, new_kv_ref[s]) for s in range(STEPS)]
    row_s = (iota((rows, 1), 0) >> 2) & 1
    row_g = iota((rows, 1), 0) & 3
    lengths = jnp.sum(
        jnp.where(
            (iota((rows, seqs), 0) >> 3) == iota((rows, seqs), 1), len_ref[...].astype(F32), 0.0
        ),
        axis=1,
        keepdims=True,
    )
    sink = jnp.sum(
        jnp.where(row_g == iota((rows, GROUP), 1), sink_ref[...], 0.0), axis=1, keepdims=True
    )
    scale = HD**-0.5
    batched = (((2,), (2,)), ((0,), (0,)))
    scores = (
        lax.dot_general(
            spread_q.reshape(seqs, STEPS * GROUP, lanes).astype(BF),
            band_ref[...],
            batched,
            preferred_element_type=F32,
        ).reshape(rows, -1)
        * scale
    )
    window = band_ref.shape[1]
    w_id = iota((rows, window), 1)
    kept = (w_id >= row_s + 1) & (w_id.astype(F32) >= window - lengths)
    scores = jnp.where(kept, scores, -1e30)
    new_scores = [
        jnp.sum(spread_q * fresh[s], axis=1, keepdims=True) * scale for s in range(STEPS)
    ]
    new_scores[1] = jnp.where(row_s == 1, new_scores[1], -1e30)
    top = jnp.maximum(jnp.max(scores, axis=1, keepdims=True), sink)
    top = jnp.maximum(jnp.maximum(top, new_scores[0]), new_scores[1])
    raised = jnp.exp(scores - top)
    new_raised = [jnp.exp(n - top) for n in new_scores]
    total = jnp.sum(raised, axis=1, keepdims=True) + jnp.exp(sink - top)
    total = total + new_raised[0] + new_raised[1]
    probs = (raised / total).reshape(seqs, STEPS * GROUP, window).astype(BF)
    mixed = lax.dot_general(
        probs, band_ref[...], (((2,), (1,)), ((0,), (0,))), preferred_element_type=F32
    ).reshape(rows, lanes)
    for s in range(STEPS):
        mixed += (new_raised[s] / total).astype(BF).astype(F32) * fresh[s]
    mixed = mixed.astype(BF)
    attended = jnp.zeros((cols, GROUP * HD), F32)
    for g in range(GROUP):
        l_id = iota((lanes, GROUP * HD), 0)
        k_id = iota((lanes, GROUP * HD), 1)
        pick = ((k_id - g * HD == l_id - HD) & (l_id >= HD)).astype(BF)
        part = dot(mixed, pick).astype(BF)
        attended += dot((same_t & ((rt_id & 3) == g)).astype(BF), part)
    attended = attended.astype(BF)

    for j in range(n_head):
        part_out[j] = dot(attended, o_ref[j * share : (j + 1) * share, :], ((1,), (1,))).astype(BF)

    def send_part(i, carry):
        to = lax.rem(head + i, n_head)
        send(part_out.at[to], part_in.at[head], me, to, sem.at[PART_S], sem.at[PART_R])
        return carry

    lax.fori_loop(1, n_head, send_part, 0)
    part_in[head] = part_out[head]

    new_col = column(new_ref[...].astype(F32), experts)
    logits = [logit_ref[j : j + 1, :] for j in range(TOP)]
    highest = functools.reduce(jnp.maximum, logits)
    powers = [jnp.exp(l - highest) for l in logits]
    power_sum = functools.reduce(jnp.add, powers)
    member = jnp.zeros((experts, cols), F32)
    weight = jnp.zeros((experts, cols), F32)
    for j in range(TOP):
        hit = (route_ref[j : j + 1, :].astype(F32) == new_col).astype(F32)
        member += hit
        weight += hit * (powers[j] / power_sum)
    u0 = iota((cols, cols), 0)
    u1 = iota((cols, cols), 1)
    before = ((u0 < u1) & ((u0 >> seq_bits) == (u1 >> seq_bits))).astype(BF)
    rank = dot(member.astype(BF), before)
    slots = experts * ROWS
    of_slot = ((iota((slots, experts), 0) >> 4) == iota((slots, experts), 1)).astype(BF)
    member_rows = dot(of_slot, member.astype(BF))
    rank_rows = dot(of_slot, rank.astype(BF))
    i_id = iota((slots, cols), 0)
    place = (
        member_rows
        * (rank_rows == (i_id & 7).astype(F32)).astype(F32)
        * (((i_id >> 3) & 1) == (iota((slots, cols), 1) >> seq_bits)).astype(F32)
    )
    combine = dot(of_slot.astype(F32), weight, precision=EXACT) * place

    drain(part_in.at[pl.ds(0, n_head - 1)], sem.at[PART_R])
    hidden = residual_ref[...].reshape(cols, share).astype(F32)
    for j in range(n_head):
        hidden += part_in[j].astype(F32)
    squares = jnp.sum(hidden * hidden, axis=1, keepdims=True)
    lane = iota((share, wide), 1)
    stretch = jnp.zeros((share, wide), F32)
    gap = jnp.zeros((share, wide), jnp.int32)
    for b in range(1, per_head):
        gap += pad * (iota((share, wide), 0) >= b * block).astype(jnp.int32)
    stretch = (iota((share, wide), 0) + gap == lane).astype(BF)
    gained = (hidden * gain_ref[pl.ds(head, 1), :]).astype(BF)
    token = dot(gained, stretch)
    high = squares.astype(BF).astype(F32)
    low = (squares - high).astype(BF).astype(F32)
    lane = iota((cols, wide), 1)
    token = jnp.where(lane == block, high, jnp.where(lane == block + 1, low, token)).astype(BF)
    tok_out[...] = dot(place.astype(BF), token).astype(BF).reshape(experts, ROWS, wide)

    def send_token(i, carry):
        slot = lax.rem(my_slot + i, experts)
        for p in range(2):
            send(
                tok_out.at[slot],
                tok_all.at[head, me],
                2 * slot + p,
                head,
                sem.at[TOK_S],
                sem.at[TOK_R],
            )
        return carry

    send(tok_out.at[my_slot], tok_all.at[head, me], partner, head, sem.at[TOK_S], sem.at[TOK_R])
    tok_all[head, me] = tok_out[my_slot]
    lax.fori_loop(1, experts, send_token, 0)

    lax.fori_loop(first_batch, experts, send_gate_up, 0)
    lax.fori_loop(1, experts, send_down, 0)

    drain(tok_all.at[head, pl.ds(0, n_expert - 1)], sem.at[TOK_R])
    per = n_expert // CHUNKS

    def chunk(k):
        return pl.ds(k * per, per)

    for k in range(CHUNKS):
        for d in range(1, n_chip):
            to = 2 * lax.rem(chip + d, n_chip) + core
            view = tok_all.at[head, chunk(k)]
            send(view, view, me, to, sem.at[AG_S], ag_sem.at[k, head])
        view = tok_all.at[head, chunk(k)]
        send(view, view, me, mate, sem.at[AG_S], ag_sem.at[k, head])
    for k in range(CHUNKS):
        for d in range(1, n_chip):
            source = 2 * lax.rem(chip + n_chip - d, n_chip) + core
            view = tok_all.at[source, chunk(k)]
            drain(view, ag_sem.at[k, source])
            send(view, view, me, mate, sem.at[AG_S], ag_sem.at[k, source])

    drain(gu_in.at[pl.ds(0, n_expert - 1)], sem.at[GU_R])
    drain(dn_in.at[pl.ds(0, n_expert - 1)], sem.at[DN_R])

    size = per * ROWS
    q_id = iota((wide, half), 0)
    pick = ((q_id == block) | (q_id == block + 1)).astype(BF)

    def run(k):
        for x in range(n_chip):
            source = 2 * x + 1 - core
            drain(tok_all.at[source, chunk(k)], ag_sem.at[k, source])
        acc = jnp.zeros((size, 2 * half), F32)
        norm = jnp.zeros((size, half), F32)
        for j in range(0, n_head, 2):
            pair = [tok_all[j + i, chunk(k)].reshape(size, wide) for i in range(2)]
            weights = gu_in[per_head * j : per_head * (j + 2)].reshape(2 * wide, 2 * half)
            acc += dot(jnp.concatenate(pair, axis=1), weights)
            for one in pair:
                norm += dot(one[:, : min(wide, 128)], pick[: min(wide, 128)])
        norm = lax.rsqrt(norm * (1.0 / width) + EPSILON)
        gate = jnp.minimum(acc[:, :half] * norm, 7.0)
        up = jnp.clip(acc[:, half:] * norm, -7.0, 7.0)
        active = ((up + 1.0) * gate * jax.nn.sigmoid(1.702 * gate)).astype(BF)
        for j in range(n_head):
            weights = dn_in[per_head * j : per_head * (j + 1)].reshape(wide, half)
            y = dot(active, weights, ((1,), (1,))).astype(BF)
            y_out[j // 2, j % 2, chunk(k)] = y.reshape(per, ROWS, wide)
        send(
            y_out.at[:, 1 - core, chunk(k)],
            y_in.at[:, chunk(k)],
            me,
            mate,
            sem.at[Y_S],
            rs_sem.at[k, 0],
        )

    def add_cores(k):
        drain(y_in.at[:, chunk(k)], rs_sem.at[k, 0])
        for d in range(n_chip):
            to = lax.rem(chip + d, n_chip)
            z = y_out[to, core, chunk(k)].astype(F32) + y_in[to, chunk(k)].astype(F32)
            z_out[to, chunk(k)] = z.astype(BF)
            if d > 0:
                send(
                    z_out.at[to, chunk(k)],
                    z_in.at[d - 1, chunk(k)],
                    me,
                    2 * to + core,
                    sem.at[Z_S],
                    rs_sem.at[k, d],
                )

    def add_chips(k):
        total = z_out[chip, chunk(k)].astype(F32)
        for d in range(1, n_chip):
            drain(z_in.at[d - 1, chunk(k)], rs_sem.at[k, d])
            total += z_in[d - 1, chunk(k)].astype(F32)
        ret_out[chunk(k)] = total.astype(BF)

        def give_back(i, carry):
            to = k * per + lax.rem(me + i, per)

            @pl.when(to != me)
            def _():
                send(ret_out.at[to], ret_in.at[me], to, head, sem.at[RET_S], sem.at[RET_R])

            @pl.when(to == me)
            def _():
                ret_in[me] = ret_out[me]

            return carry

        lax.fori_loop(0, per, give_back, 0)

    for k in range(CHUNKS):
        run(k)
        if k > 0:
            add_cores(k - 1)
        if k > 1:
            add_chips(k - 2)
    add_cores(CHUNKS - 1)
    if CHUNKS > 1:
        add_chips(CHUNKS - 2)

    for i in range(n_expert):
        sync_f[i * block : (i + 1) * block, :] = dn_in[i].astype(F32)[:block]
    sync_ref[...] = sync_f[...].astype(BF)
    add_chips(CHUNKS - 1)

    drain(ret_in.at[pl.ds(0, n_expert - 1)], sem.at[RET_R])
    returned = ret_in[...].astype(F32).reshape(experts, 2, ROWS, wide)
    returned = (returned[:, 0] + returned[:, 1]).reshape(slots, wide)
    mix = dot(combine, returned, ((0,), (0,)), precision=EXACT)
    mix = dot(mix, stretch.astype(F32), ((1,), (1,)), precision=EXACT)
    out_ref[...] = (hidden + mix).astype(BF).reshape(STEPS, seqs, share)

    drain(gu_in.at[pl.ds(0, n_expert - 1)], sem.at[GU_S])
    drain(dn_in.at[pl.ds(0, n_expert - 1)], sem.at[DN_S])
    drain(part_in.at[pl.ds(0, n_head - 1)], sem.at[PART_S])
    drain(tok_all.at[0, pl.ds(0, n_expert - 1)], sem.at[TOK_S])
    drain(ret_in.at[pl.ds(0, n_expert - 1)], sem.at[RET_S])
    drain(tok_all.at[pl.ds(0, n_head - 1)], sem.at[AG_S])
    drain(y_in, sem.at[Y_S])
    drain(z_in, sem.at[Z_S])


def local(
    n_expert,
    n_head,
    queries,
    cache_band,
    new_kv,
    cache_lengths,
    sink_logits,
    o_weight,
    residual,
    norm_gain,
    route_logits,
    routes,
    old_experts,
    new_experts,
    train_gate_up,
    train_down,
):
    experts = old_experts.shape[0]
    seqs = queries.shape[1]
    cols = STEPS * seqs
    block = train_gate_up.shape[1]
    padded = -(-block // 16) * 16
    share = residual.shape[2]
    wide = n_expert // n_head * padded
    half = train_gate_up.shape[3] // 2
    n_chip = n_head // 2
    width = norm_gain.shape[0]
    counter = jnp.arange(experts, dtype=jnp.int32)
    position = jnp.sum(
        jnp.where(old_experts[None, :] == new_experts[:, None], counter[None, :], 0), axis=1
    )
    logits = jnp.transpose(route_logits, (2, 0, 1)).reshape(TOP, cols)
    choices = jnp.transpose(routes, (2, 0, 1)).reshape(TOP, cols)
    vmem = pl.BlockSpec(memory_space=pltpu.VMEM)
    out, synced = pl.pallas_call(
        functools.partial(kernel, n_expert, n_head),
        out_shape=(
            jax.ShapeDtypeStruct((STEPS, seqs, share), BF),
            jax.ShapeDtypeStruct((width, half), BF),
        ),
        in_specs=[pl.BlockSpec(memory_space=pltpu.SMEM)] + [vmem] * 13,
        out_specs=(vmem, vmem),
        scratch_shapes=[
            pltpu.VMEM((2, block * experts, half), F32),
            pltpu.VMEM((experts, 2, padded, 2 * half), BF),
            pltpu.VMEM((experts, 2, padded, half), BF),
            pltpu.VMEM((n_expert, padded, 2 * half), BF),
            pltpu.VMEM((n_expert, padded, half), BF),
            pltpu.VMEM((n_head, cols, share), BF),
            pltpu.VMEM((n_head, cols, share), BF),
            pltpu.VMEM((experts, ROWS, wide), BF),
            pltpu.VMEM((n_head, n_expert, ROWS, wide), BF),
            pltpu.VMEM((n_chip, 2, n_expert, ROWS, wide), BF),
            pltpu.VMEM((n_chip, n_expert, ROWS, wide), BF),
            pltpu.VMEM((n_chip, n_expert, ROWS, wide), BF),
            pltpu.VMEM((n_chip - 1, n_expert, ROWS, wide), BF),
            pltpu.VMEM((n_expert, ROWS, wide), BF),
            pltpu.VMEM((n_expert, ROWS, wide), BF),
            pltpu.VMEM((width, half), F32),
            pltpu.SemaphoreType.DMA((13,)),
            pltpu.SemaphoreType.DMA((CHUNKS, n_head)),
            pltpu.SemaphoreType.DMA((CHUNKS, n_chip)),
        ],
        compiler_params=pltpu.CompilerParams(
            collective_id=0, has_side_effects=True, vmem_limit_bytes=56 << 20
        ),
    )(
        position,
        new_experts.reshape(1, -1),
        cache_lengths.reshape(1, -1),
        sink_logits.reshape(1, -1),
        logits,
        choices,
        norm_gain.reshape(n_head, share),
        queries,
        cache_band,
        new_kv,
        o_weight.T,
        residual,
        train_gate_up,
        jnp.transpose(train_down, (1, 0, 2)),
    )
    return out, synced[None]


def solution(mesh):
    in_specs = (
        P(None, "expert", "head"),
        P("expert", None, "head"),
        P(None, "expert", "head"),
        P("expert"),
        P("head"),
        P("head", None),
        P(None, "expert", "head"),
        P(),
        P(None, "expert", None),
        P(None, "expert", None),
        P(),
        P(),
        P(None, "expert", None, "head"),
        P(None, "expert", "head"),
    )
    out_specs = (P(None, "expert", "head"), P("expert", None, "head"))
    body = functools.partial(local, mesh.shape["expert"], mesh.shape["head"])
    return jax.shard_map(body, mesh=mesh, in_specs=in_specs, out_specs=out_specs, check_vma=False)
```

time: 471 us -> 185 us (0.39); the launches traced: 463 us -> 183 us
  waiting for transfers between devices: 267 us -> 0 us
  Pallas kernels: 0 us -> 173 us
  starting transfers between devices: 78.1 us -> 0 us
  local copies, waits for them, and re-layouts: 61.9 us -> 7.55 us
  matrix products: 21.5 us -> 0 us
  other arithmetic: 19.9 us -> 1.34 us
  between operations: 14.5 us -> 0.64 us
    pallas_call x0 -> x1, Pallas kernels: none -> 173 us  [local(): pl.pallas_call(functools.partial(kernel, n_expert, n_head), out_shape=(ja...]
    all_to_all x5 -> x0, waiting for transfers between devices: 147 us -> none  [the longest x1 118 us: local(): lax.all_to_all(stacked, 'expert', split_axis=0, concat_axis=1, tiled=True)]
    all_to_all x5 -> x0, starting transfers between devices: 77.7 us -> none  [the longest x2 40.5 us: local(): lax.all_to_all(outgoing, 'expert', split_axis=0, concat_axis=0, tiled=True)]
    psum x1 -> x0, waiting for transfers between devices: 73.1 us -> none  [local(): hidden = lax.psum(placed.astype(jnp.bfloat16), 'head').astype(jnp.float32)]
    reduce_scatter x2 -> x0, waiting for transfers between devices: 46.6 us -> none  [local(): lax.psum_scatter(partial_out.astype(jnp.float32).astype(jnp.bfloat16), 'h...]
    dot_general x14 -> x0, matrix products: 21.5 us -> none  [the longest x2 6.67 us: local(): jnp.einsum('rd,dcf->rcf', token_rows, weight_in, preferred_element_type=j...]
    gather x5 -> x0, local copies, waits for them, and re-layouts: 18 us -> none  [the longest x1 8.82 us: local(): train_gate_up[dest_pos]]
    concatenate x2 -> x0, other arithmetic: 11.7 us -> none  [the longest x1 8.8 us: local(): jnp.concatenate([train_gate_up[dest_pos], train_down[dest_pos][:, :, None...]
  transfers between devices with their start and end apart: 8 -> 0, of which waited for: 7 -> 0; matrix products, arithmetic and copies ran while one was open for 17% -> 0% of each run, Pallas kernels for 0% -> 0%
where the time goes in v1:
time: 185 us; the launch traced here: 183 us
  Pallas kernels  173 us (94%)
  local copies, waits for them, and re-layouts  7.55 us (4%)
    pallas_call x1, Pallas kernels, local(): pl.pallas_call(functools.partial(kernel, n_expert, n_head), out_shape=(ja...  173 us

profile of v1, /device:TPU:56, one launch (start us, length us, event | category | flops | bytes accessed | tf_op | source)
XLA Modules:
  0.0 182.7 jit_solution(14208284534932654808)
XLA Ops:
  0.6 1.3 select_reduce_fusion.pos_ref
  2.0 0.7 copy.18
  2.7 0.7 reshape.27.logit_ref
  3.3 0.7 copy.19
  4.0 0.7 reshape.28.route_ref
  4.7 1.4 reshape.29.gain_ref
  6.1 173.2 %shard_map.149 = (bf16[2,32,360]{2,1,0:T(8,128)(2,1)}, bf16[2880,128]{1,0:T(8,128)(2,1)}) custom-call(s32[32]{0:T(128)} %select_reduce_fusion.pos_ref, s32[1,32]{1,0:T(1,128)} %bitcast.13, s32[1,32]{1,0:T(1,128)} %bitcast.14, f32[1,4]{1,0:T(1,128)} %bitcast.15, f32[4,64]{1,0:T(4,128)} %reshape.27.logit_ref, s32[4,64]{1,0:T(4,128)} %reshape.28.route_ref, ...), custom_call_target="tpu_custom_call" | custom-call | tf_op jit(solution)/shard_map/pallas_call | solution.py:492
  179.3 1.4 copy.22
  180.7 2.0 %copy.23 = bf16[1,2880,128]{2,1,0:T(8,128)(2,1)} copy(bf16[1,2880,128]{2,1,0:T(8,128)(2,1)} %bitcast.10) | data formatting | bytes 1474560

commit v2 on v1

--- a/solution.py
+++ b/solution.py
@@ -14,6 +14,9 @@
 ROWS = STEPS * CAP
 EPSILON = 1e-05
 CHUNKS = 4
+STRIDE = 11
+FIRST_BATCH = 12
+DOWN_EARLY = 16
 MESH = pl.DeviceIdType.MESH
 BF = jnp.bfloat16
 F32 = jnp.float32
@@ -64,17 +67,26 @@
     dn_in,
     part_out,
     part_in,
+    square_out,
+    square_in,
     tok_out,
     tok_all,
+    half_f,
+    half_out,
+    half_in,
+    act_all,
     y_out,
     y_in,
     z_out,
     z_in,
     ret_out,
     ret_in,
+    sync_in,
     sync_f,
     sem,
+    tok_sem,
     ag_sem,
+    pair_sem,
     rs_sem,
 ):
     experts = n_expert // 2
@@ -87,8 +99,10 @@
     per_head = n_expert // n_head
     wide = per_head * padded
     width = n_head * share
-    half = gate_up_ref.shape[3] // 2
+    units = gate_up_ref.shape[3]
+    half = units // 2
     seq_bits = log2(seqs)
+    per = n_expert // CHUNKS
 
     me = lax.axis_index("expert")
     head = lax.axis_index("head")
@@ -96,8 +110,15 @@
     chip = head // 2
     mate = head + 1 - 2 * core
     my_slot = me // 2
-    partner = me + 1 - 2 * lax.rem(me, 2)
-    my_half = lax.rem(me, 2)
+    my_side = lax.rem(me, 2)
+    partner = me + 1 - 2 * my_side
+    row_head = me // per_head
+    row_side = lax.rem(row_head, 2)
+    row_index = (row_head // 2) * per_head + lax.rem(me, per_head)
+    my_chunk = lax.rem(me + me // (2 * CHUNKS), CHUNKS)
+    my_spot = my_chunk * per + me // CHUNKS
+    gathers = my_side == core
+    keeps_rows = my_side == row_side
 
     barrier = pltpu.get_barrier_semaphore()
 
@@ -121,13 +142,12 @@
             down_ref[:, :, p * half : (p + 1) * half].astype(F32).reshape(block * experts, half)
         )
     pad = padded - block
-    tail = padded - 16 if padded >= 16 else 0
-    gu_out[:, :, tail:, :] = jnp.zeros((experts, 2, padded - tail, 2 * half), BF)
-    dn_out[:, :, tail:, :] = jnp.zeros((experts, 2, padded - tail, half), BF)
-
-    pl.semaphore_wait(barrier, n_expert + n_head - 2)
-
-    GU_S, GU_R, DN_S, DN_R, PART_S, PART_R, TOK_S, TOK_R, RET_S, RET_R, AG_S, Y_S, Z_S = range(13)
+    last = padded - 16
+    gu_out[:, last:, :] = jnp.zeros((experts, 16, 2 * units), BF)
+    dn_out[:, last:, :] = jnp.zeros((experts, 16, units), BF)
+
+    GU_S, GU_R, DN_S, DN_R, PART_S, PART_R, SQ_S, SQ_R = range(8)
+    TOK_S, AG_S, HALF_S, ACT_S, Y_S, Z_S, RET_S, RET_R, SYNC_S, SYNC_R = range(8, 18)
 
     def send(src, dst, e, h, s, r):
         pltpu.make_async_remote_copy(
@@ -144,41 +164,33 @@
 
     def prepare_gate_up(slot):
         index = pos_ref[slot]
-        for p in range(2):
-            for c in range(2):
-                gu_out[slot, p, :block, c * half : (c + 1) * half] = gate_up_ref[
-                    index, :, c, p * half : (p + 1) * half
-                ]
+        for c in range(2):
+            gu_out[slot, :block, c * units : (c + 1) * units] = gate_up_ref[index, :, c, :]
 
     def prepare_down(slot):
         index = pos_ref[slot]
         for p in range(2):
-            dn_out[slot, p, :block, :] = down_f[
+            dn_out[slot, :block, p * half : (p + 1) * half] = down_f[
                 p, pl.ds(index, block, stride=experts), :
             ].astype(BF)
 
+    def order(i):
+        step = lax.rem(i * STRIDE, experts)
+        return lax.rem(my_slot + jnp.where(core == 0, step, experts - step), experts)
+
     def send_gate_up(i, carry):
-        slot = lax.rem(my_slot + i, experts)
+        slot = order(i)
         prepare_gate_up(slot)
-        for p in range(2):
-            send(gu_out.at[slot, p], gu_in.at[me], 2 * slot + p, head, sem.at[GU_S], sem.at[GU_R])
+        to = 2 * slot + row_side
+        send(gu_out.at[slot], gu_in.at[row_index], to, head, sem.at[GU_S], sem.at[GU_R])
         return carry
 
     def send_down(i, carry):
-        slot = lax.rem(my_slot + i, experts)
+        slot = order(i)
         prepare_down(slot)
-        for p in range(2):
-            send(dn_out.at[slot, p], dn_in.at[me], 2 * slot + p, head, sem.at[DN_S], sem.at[DN_R])
+        to = 2 * slot + row_side
+        send(dn_out.at[slot], dn_in.at[row_index], to, head, sem.at[DN_S], sem.at[DN_R])
         return carry
-
-    prepare_gate_up(my_slot)
-    prepare_down(my_slot)
-    send(gu_out.at[my_slot, 1 - my_half], gu_in.at[me], partner, head, sem.at[GU_S], sem.at[GU_R])
-    send(dn_out.at[my_slot, 1 - my_half], dn_in.at[me], partner, head, sem.at[DN_S], sem.at[DN_R])
-    gu_in[me] = gu_out[my_slot, my_half]
-    dn_in[me] = dn_out[my_slot, my_half]
-    first_batch = experts // 2
-    lax.fori_loop(1, first_batch, send_gate_up, 0)
 
     lanes = 2 * HD
     rows = STEPS * GROUP * seqs
@@ -254,6 +266,8 @@
     for j in range(n_head):
         part_out[j] = dot(attended, o_ref[j * share : (j + 1) * share, :], ((1,), (1,))).astype(BF)
 
+    pl.semaphore_wait(barrier, n_expert + n_head - 2)
+
     def send_part(i, carry):
         to = lax.rem(head + i, n_head)
         send(part_out.at[to], part_in.at[head], me, to, sem.at[PART_S], sem.at[PART_R])
@@ -261,6 +275,25 @@
 
     lax.fori_loop(1, n_head, send_part, 0)
     part_in[head] = part_out[head]
+
+    prepare_gate_up(my_slot)
+    prepare_down(my_slot)
+
+    @pl.when(keeps_rows)
+    def _():
+        pltpu.make_async_copy(gu_out.at[my_slot], gu_in.at[row_index], sem.at[GU_R]).start()
+        pltpu.make_async_copy(dn_out.at[my_slot], dn_in.at[row_index], sem.at[DN_R]).start()
+
+    @pl.when(jnp.logical_not(keeps_rows))
+    def _():
+        send(
+            gu_out.at[my_slot], gu_in.at[row_index], partner, head, sem.at[GU_S], sem.at[GU_R]
+        )
+        send(
+            dn_out.at[my_slot], dn_in.at[row_index], partner, head, sem.at[DN_S], sem.at[DN_R]
+        )
+
+    lax.fori_loop(1, FIRST_BATCH, send_gate_up, 0)
 
     new_col = column(new_ref[...].astype(F32), experts)
     logits = [logit_ref[j : j + 1, :] for j in range(TOP)]
@@ -294,101 +327,171 @@
     for j in range(n_head):
         hidden += part_in[j].astype(F32)
     squares = jnp.sum(hidden * hidden, axis=1, keepdims=True)
+    square_row = jnp.sum(
+        jnp.where(iota((cols, cols), 0) == iota((cols, cols), 1), squares, 0.0),
+        axis=0,
+        keepdims=True,
+    )
+    square_out[...] = jnp.broadcast_to(square_row, square_out.shape)
+
+    def send_square(i, carry):
+        to = lax.rem(head + i, n_head)
+        send(square_out, square_in.at[head], me, to, sem.at[SQ_S], sem.at[SQ_R])
+        return carry
+
+    lax.fori_loop(1, n_head, send_square, 0)
+    square_in[head] = square_out[...]
     lane = iota((share, wide), 1)
-    stretch = jnp.zeros((share, wide), F32)
     gap = jnp.zeros((share, wide), jnp.int32)
     for b in range(1, per_head):
         gap += pad * (iota((share, wide), 0) >= b * block).astype(jnp.int32)
     stretch = (iota((share, wide), 0) + gap == lane).astype(BF)
-    gained = (hidden * gain_ref[pl.ds(head, 1), :]).astype(BF)
-    token = dot(gained, stretch)
-    high = squares.astype(BF).astype(F32)
-    low = (squares - high).astype(BF).astype(F32)
-    lane = iota((cols, wide), 1)
-    token = jnp.where(lane == block, high, jnp.where(lane == block + 1, low, token)).astype(BF)
+    gained = hidden * gain_ref[pl.ds(head, 1), :]
+    drain(square_in.at[pl.ds(0, n_head - 1)], sem.at[SQ_R])
+    all_squares = jnp.zeros((1, cols), F32)
+    for j in range(n_head):
+        all_squares += square_in[j, 0:1, :]
+    norm = column(lax.rsqrt(all_squares * (1.0 / width) + EPSILON), cols)
+    token = dot((gained * norm).astype(BF), stretch).astype(BF)
     tok_out[...] = dot(place.astype(BF), token).astype(BF).reshape(experts, ROWS, wide)
 
     def send_token(i, carry):
-        slot = lax.rem(my_slot + i, experts)
-        for p in range(2):
-            send(
-                tok_out.at[slot],
-                tok_all.at[head, me],
-                2 * slot + p,
-                head,
-                sem.at[TOK_S],
-                sem.at[TOK_R],
-            )
+        slot = order(i)
+        send(
+            tok_out.at[slot],
+            tok_all.at[chip, my_spot],
+            2 * slot + core,
+            head,
+            sem.at[TOK_S],
+            tok_sem.at[my_chunk],
+        )
         return carry
 
-    send(tok_out.at[my_slot], tok_all.at[head, me], partner, head, sem.at[TOK_S], sem.at[TOK_R])
-    tok_all[head, me] = tok_out[my_slot]
+    @pl.when(gathers)
+    def _():
+        pltpu.make_async_copy(
+            tok_out.at[my_slot], tok_all.at[chip, my_spot], tok_sem.at[my_chunk]
+        ).start()
+
+    @pl.when(jnp.logical_not(gathers))
+    def _():
+        send(
+            tok_out.at[my_slot],
+            tok_all.at[chip, my_spot],
+            partner,
+            head,
+            sem.at[TOK_S],
+            tok_sem.at[my_chunk],
+        )
+
     lax.fori_loop(1, experts, send_token, 0)
 
-    lax.fori_loop(first_batch, experts, send_gate_up, 0)
-    lax.fori_loop(1, experts, send_down, 0)
-
-    drain(tok_all.at[head, pl.ds(0, n_expert - 1)], sem.at[TOK_R])
-    per = n_expert // CHUNKS
+    def feed(sent, count, limit):
+        while count and sent[0] < experts:
+            n = min(count, experts - sent[0])
+            lax.fori_loop(sent[0], sent[0] + n, send_gate_up, 0)
+            sent[0] += n
+            count -= n
+        n = min(count, limit - sent[1])
+        if n > 0:
+            lax.fori_loop(sent[1], sent[1] + n, send_down, 0)
+            sent[1] += n
 
     def chunk(k):
         return pl.ds(k * per, per)
 
+    @pl.when(gathers)
+    def _():
+        sent = [FIRST_BATCH, 1]
+        feed(sent, 8, DOWN_EARLY)
+        for k in range(CHUNKS):
+            view = tok_all.at[chip, chunk(k)]
+            drain(view, tok_sem.at[k])
+            for d in range(1, n_chip):
+                to = 2 * lax.rem(chip + d, n_chip) + core
+                send(view, view, me, to, sem.at[AG_S], ag_sem.at[k, chip])
+            send(view, view, me, mate, sem.at[AG_S], ag_sem.at[k, chip])
+            feed(sent, 2, DOWN_EARLY)
+        for k in range(CHUNKS):
+            for d in range(1, n_chip):
+                source = lax.rem(chip + n_chip - d, n_chip)
+                view = tok_all.at[source, chunk(k)]
+                drain(view, ag_sem.at[k, source])
+                send(view, view, me, mate, sem.at[AG_S], ag_sem.at[k, source])
+            feed(sent, 5, DOWN_EARLY)
+        feed(sent, 2 * experts, DOWN_EARLY)
+
+    @pl.when(jnp.logical_not(gathers))
+    def _():
+        feed([FIRST_BATCH, 1], 2 * experts, DOWN_EARLY)
+        for k in range(CHUNKS):
+            for source in range(n_chip):
+                drain(tok_all.at[source, chunk(k)], ag_sem.at[k, source])
+
+    drain(gu_in, sem.at[GU_R])
+    size = per * ROWS
+    part_size = size // 2
+    sent = [experts, DOWN_EARLY]
     for k in range(CHUNKS):
-        for d in range(1, n_chip):
-            to = 2 * lax.rem(chip + d, n_chip) + core
-            view = tok_all.at[head, chunk(k)]
-            send(view, view, me, to, sem.at[AG_S], ag_sem.at[k, head])
-        view = tok_all.at[head, chunk(k)]
-        send(view, view, me, mate, sem.at[AG_S], ag_sem.at[k, head])
+        acc = jnp.zeros((size, 2 * units), F32)
+        for j in range(0, n_chip, 2):
+            rows_in = jnp.concatenate(
+                [tok_all[j + i, chunk(k)].reshape(size, wide) for i in range(2)], axis=1
+            )
+            weights = gu_in[per_head * j : per_head * (j + 2)].reshape(2 * wide, 2 * units)
+            acc += dot(rows_in, weights)
+        for p in range(2):
+            piece = acc[p * part_size : (p + 1) * part_size]
+            half_f[k, p] = piece
+            half_out[k, p] = piece.astype(BF)
+        send(
+            half_out.at[k, 1 - my_side],
+            half_in.at[k],
+            partner,
+            head,
+            sem.at[HALF_S],
+            pair_sem.at[k, 0],
+        )
+        feed(sent, experts // CHUNKS, experts)
+    feed(sent, experts, experts)
     for k in range(CHUNKS):
-        for d in range(1, n_chip):
-            source = 2 * lax.rem(chip + n_chip - d, n_chip) + core
-            view = tok_all.at[source, chunk(k)]
-            drain(view, ag_sem.at[k, source])
-            send(view, view, me, mate, sem.at[AG_S], ag_sem.at[k, source])
-
-    drain(gu_in.at[pl.ds(0, n_expert - 1)], sem.at[GU_R])
-    drain(dn_in.at[pl.ds(0, n_expert - 1)], sem.at[DN_R])
-
-    size = per * ROWS
-    q_id = iota((wide, half), 0)
-    pick = ((q_id == block) | (q_id == block + 1)).astype(BF)
+        drain(half_in.at[k], pair_sem.at[k, 0])
+        acc = half_f[k, my_side] + half_in[k].astype(F32)
+        gate = jnp.minimum(acc[:, :units], 7.0)
+        up = jnp.clip(acc[:, units:], -7.0, 7.0)
+        active = (up + 1.0) * gate * jax.nn.sigmoid(1.702 * gate)
+        act_all[my_side, k] = active.astype(BF)
+        view = act_all.at[my_side, k]
+        send(view, view, partner, head, sem.at[ACT_S], pair_sem.at[k, 1])
+
+    drain(dn_in, sem.at[DN_R])
+    lanes_out = pl.ds(pl.multiple_of((1 - my_side) * half, half), half)
+    lanes_own = pl.ds(pl.multiple_of(my_side * half, half), half)
 
     def run(k):
-        for x in range(n_chip):
-            source = 2 * x + 1 - core
-            drain(tok_all.at[source, chunk(k)], ag_sem.at[k, source])
-        acc = jnp.zeros((size, 2 * half), F32)
-        norm = jnp.zeros((size, half), F32)
-        for j in range(0, n_head, 2):
-            pair = [tok_all[j + i, chunk(k)].reshape(size, wide) for i in range(2)]
-            weights = gu_in[per_head * j : per_head * (j + 2)].reshape(2 * wide, 2 * half)
-            acc += dot(jnp.concatenate(pair, axis=1), weights)
-            for one in pair:
-                norm += dot(one[:, : min(wide, 128)], pick[: min(wide, 128)])
-        norm = lax.rsqrt(norm * (1.0 / width) + EPSILON)
-        gate = jnp.minimum(acc[:, :half] * norm, 7.0)
-        up = jnp.clip(acc[:, half:] * norm, -7.0, 7.0)
-        active = ((up + 1.0) * gate * jax.nn.sigmoid(1.702 * gate)).astype(BF)
-        for j in range(n_head):
-            weights = dn_in[per_head * j : per_head * (j + 1)].reshape(wide, half)
+        drain(act_all.at[1 - my_side, k], pair_sem.at[k, 1])
+        active = jnp.concatenate([act_all[0, k], act_all[1, k]], axis=0)
+        for j in range(n_chip):
+            weights = dn_in[per_head * j : per_head * (j + 1)].reshape(wide, units)
             y = dot(active, weights, ((1,), (1,))).astype(BF)
-            y_out[j // 2, j % 2, chunk(k)] = y.reshape(per, ROWS, wide)
-        send(
-            y_out.at[:, 1 - core, chunk(k)],
-            y_in.at[:, chunk(k)],
-            me,
-            mate,
-            sem.at[Y_S],
-            rs_sem.at[k, 0],
-        )
+            y_out[j, chunk(k)] = y.reshape(per, ROWS, wide)
+
+        @pl.when(jnp.logical_not(gathers))
+        def _():
+            send(
+                y_out.at[:, chunk(k)],
+                y_in.at[:, chunk(k)],
+                me,
+                mate,
+                sem.at[Y_S],
+                rs_sem.at[k, 0],
+            )
 
     def add_cores(k):
         drain(y_in.at[:, chunk(k)], rs_sem.at[k, 0])
         for d in range(n_chip):
             to = lax.rem(chip + d, n_chip)
-            z = y_out[to, core, chunk(k)].astype(F32) + y_in[to, chunk(k)].astype(F32)
+            z = y_out[to, chunk(k)].astype(F32) + y_in[to, chunk(k)].astype(F32)
             z_out[to, chunk(k)] = z.astype(BF)
             if d > 0:
                 send(
@@ -408,15 +511,17 @@
         ret_out[chunk(k)] = total.astype(BF)
 
         def give_back(i, carry):
-            to = k * per + lax.rem(me + i, per)
+            m = lax.rem(me + 5 * i, per)
+            to = CHUNKS * m + lax.rem(k + n_expert - m // 2, CHUNKS)
+            row = ret_out.at[k * per + m]
 
             @pl.when(to != me)
             def _():
-                send(ret_out.at[to], ret_in.at[me], to, head, sem.at[RET_S], sem.at[RET_R])
+                send(row, ret_in.at[my_slot], to, head, sem.at[RET_S], sem.at[RET_R])
 
             @pl.when(to == me)
             def _():
-                ret_in[me] = ret_out[me]
+                pltpu.make_async_copy(row, ret_in.at[my_slot], sem.at[RET_R]).start()
 
             return carry
 
@@ -424,34 +529,76 @@
 
     for k in range(CHUNKS):
         run(k)
-        if k > 0:
-            add_cores(k - 1)
-        if k > 1:
-            add_chips(k - 2)
-    add_cores(CHUNKS - 1)
-    if CHUNKS > 1:
+
+        @pl.when(gathers)
+        def _():
+            if k > 0:
+                add_cores(k - 1)
+            if k > 1:
+                add_chips(k - 2)
+
+    @pl.when(gathers)
+    def _():
+        add_cores(CHUNKS - 1)
         add_chips(CHUNKS - 2)
 
+    send(
+        dn_in.at[:, :, lanes_out],
+        sync_in.at[my_side],
+        partner,
+        head,
+        sem.at[SYNC_S],
+        sem.at[SYNC_R],
+    )
+    sync_in[my_side] = dn_in[:, :, lanes_own]
+
+    @pl.when(gathers)
+    def _():
+        add_chips(CHUNKS - 1)
+
+    drain(sync_in.at[1 - my_side], sem.at[SYNC_R])
     for i in range(n_expert):
-        sync_f[i * block : (i + 1) * block, :] = dn_in[i].astype(F32)[:block]
+        h, r = divmod(i, per_head)
+        served = sync_in[h % 2, (h // 2) * per_head + r]
+        sync_f[i * block : (i + 1) * block, :] = served.astype(F32)[:block]
     sync_ref[...] = sync_f[...].astype(BF)
-    add_chips(CHUNKS - 1)
-
-    drain(ret_in.at[pl.ds(0, n_expert - 1)], sem.at[RET_R])
-    returned = ret_in[...].astype(F32).reshape(experts, 2, ROWS, wide)
-    returned = (returned[:, 0] + returned[:, 1]).reshape(slots, wide)
+
+    drain(ret_in, sem.at[RET_R])
+    returned = ret_in[...].astype(F32).reshape(slots, wide)
     mix = dot(combine, returned, ((0,), (0,)), precision=EXACT)
     mix = dot(mix, stretch.astype(F32), ((1,), (1,)), precision=EXACT)
     out_ref[...] = (hidden + mix).astype(BF).reshape(STEPS, seqs, share)
 
-    drain(gu_in.at[pl.ds(0, n_expert - 1)], sem.at[GU_S])
-    drain(dn_in.at[pl.ds(0, n_expert - 1)], sem.at[DN_S])
+    others = pl.ds(0, experts - 1)
+
+    @pl.when(keeps_rows)
+    def _():
+        drain(gu_in.at[others], sem.at[GU_S])
+        drain(dn_in.at[others], sem.at[DN_S])
+
+    @pl.when(jnp.logical_not(keeps_rows))
+    def _():
+        drain(gu_in, sem.at[GU_S])
+        drain(dn_in, sem.at[DN_S])
+
     drain(part_in.at[pl.ds(0, n_head - 1)], sem.at[PART_S])
-    drain(tok_all.at[0, pl.ds(0, n_expert - 1)], sem.at[TOK_S])
-    drain(ret_in.at[pl.ds(0, n_expert - 1)], sem.at[RET_S])
-    drain(tok_all.at[pl.ds(0, n_head - 1)], sem.at[AG_S])
-    drain(y_in, sem.at[Y_S])
-    drain(z_in, sem.at[Z_S])
+    drain(square_in.at[pl.ds(0, n_head - 1)], sem.at[SQ_S])
+    drain(half_in, sem.at[HALF_S])
+    drain(act_all.at[0], sem.at[ACT_S])
+    drain(sync_in.at[0], sem.at[SYNC_S])
+
+    @pl.when(gathers)
+    def _():
+        drain(tok_out.at[others], sem.at[TOK_S])
+        drain(tok_all, sem.at[AG_S])
+        drain(tok_all.at[pl.ds(0, n_chip - 1)], sem.at[AG_S])
+        drain(z_in, sem.at[Z_S])
+        drain(ret_out.at[pl.ds(0, n_expert - 1)], sem.at[RET_S])
+
+    @pl.when(jnp.logical_not(gathers))
+    def _():
+        drain(tok_out, sem.at[TOK_S])
+        drain(y_in, sem.at[Y_S])
 
 
 def local(
@@ -479,7 +626,9 @@
     padded = -(-block // 16) * 16
     share = residual.shape[2]
     wide = n_expert // n_head * padded
-    half = train_gate_up.shape[3] // 2
+    units = train_gate_up.shape[3]
+    half = units // 2
+    size = n_expert // CHUNKS * ROWS
     n_chip = n_head // 2
     width = norm_gain.shape[0]
     counter = jnp.arange(experts, dtype=jnp.int32)
@@ -499,23 +648,32 @@
         out_specs=(vmem, vmem),
         scratch_shapes=[
             pltpu.VMEM((2, block * experts, half), F32),
-            pltpu.VMEM((experts, 2, padded, 2 * half), BF),
-            pltpu.VMEM((experts, 2, padded, half), BF),
-            pltpu.VMEM((n_expert, padded, 2 * half), BF),
-            pltpu.VMEM((n_expert, padded, half), BF),
+            pltpu.VMEM((experts, padded, 2 * units), BF),
+            pltpu.VMEM((experts, padded, units), BF),
+            pltpu.VMEM((experts, padded, 2 * units), BF),
+            pltpu.VMEM((experts, padded, units), BF),
             pltpu.VMEM((n_head, cols, share), BF),
             pltpu.VMEM((n_head, cols, share), BF),
+            pltpu.VMEM((8, cols), F32),
+            pltpu.VMEM((n_head, 8, cols), F32),
             pltpu.VMEM((experts, ROWS, wide), BF),
-            pltpu.VMEM((n_head, n_expert, ROWS, wide), BF),
-            pltpu.VMEM((n_chip, 2, n_expert, ROWS, wide), BF),
+            pltpu.VMEM((n_chip, n_expert, ROWS, wide), BF),
+            pltpu.VMEM((CHUNKS, 2, size // 2, 2 * units), F32),
+            pltpu.VMEM((CHUNKS, 2, size // 2, 2 * units), BF),
+            pltpu.VMEM((CHUNKS, size // 2, 2 * units), BF),
+            pltpu.VMEM((2, CHUNKS, size // 2, units), BF),
+            pltpu.VMEM((n_chip, n_expert, ROWS, wide), BF),
             pltpu.VMEM((n_chip, n_expert, ROWS, wide), BF),
             pltpu.VMEM((n_chip, n_expert, ROWS, wide), BF),
             pltpu.VMEM((n_chip - 1, n_expert, ROWS, wide), BF),
             pltpu.VMEM((n_expert, ROWS, wide), BF),
-            pltpu.VMEM((n_expert, ROWS, wide), BF),
+            pltpu.VMEM((experts, ROWS, wide), BF),
+            pltpu.VMEM((2, experts, padded, half), BF),
             pltpu.VMEM((width, half), F32),
-            pltpu.SemaphoreType.DMA((13,)),
-            pltpu.SemaphoreType.DMA((CHUNKS, n_head)),
+            pltpu.SemaphoreType.DMA((18,)),
+            pltpu.SemaphoreType.DMA((CHUNKS,)),
+            pltpu.SemaphoreType.DMA((CHUNKS, n_chip)),
+            pltpu.SemaphoreType.DMA((CHUNKS, 2)),
             pltpu.SemaphoreType.DMA((CHUNKS, n_chip)),
         ],
         compiler_params=pltpu.CompilerParams(

time: 185 us -> 150 us (0.81)
  Pallas kernels: 173 us -> 139 us
    pallas_call x1, Pallas kernels: 173 us -> 139 us  [local(): pl.pallas_call(functools.partial(kernel, n_expert, n_head), out_shape=(ja...]
where the time goes in v2:
time: 150 us; the launch traced here: 148 us
  Pallas kernels  139 us (93%)
  local copies, waits for them, and re-layouts  7.55 us (5%)
    pallas_call x1, Pallas kernels, local(): pl.pallas_call(functools.partial(kernel, n_expert, n_head), out_shape=(ja...  139 us
    unnamed x2, local copies, waits for them, and re-layouts  3.45 us

profile of v2, /device:TPU:56, one launch (start us, length us, event | category | flops | bytes accessed | tf_op | source)
XLA Modules:
  0.0 148.1 jit_solution(17005037893173571689)
XLA Ops:
  0.6 1.3 select_reduce_fusion.pos_ref
  2.0 0.7 copy.18
  2.7 0.7 reshape.27.logit_ref
  3.3 0.7 copy.19
  4.0 0.7 reshape.28.route_ref
  4.7 1.4 reshape.29.gain_ref
  6.1 138.6 %shard_map.149 = (bf16[2,32,360]{2,1,0:T(8,128)(2,1)}, bf16[2880,128]{1,0:T(8,128)(2,1)}) custom-call(s32[32]{0:T(128)} %select_reduce_fusion.pos_ref, s32[1,32]{1,0:T(1,128)} %bitcast.13, s32[1,32]{1,0:T(1,128)} %bitcast.14, f32[1,4]{1,0:T(1,128)} %bitcast.15, f32[4,64]{1,0:T(4,128)} %reshape.27.logit_ref, s32[4,64]{1,0:T(4,128)} %reshape.28.route_ref, ...), custom_call_target="tpu_custom_call" | custom-call | tf_op jit(solution)/shard_map/pallas_call | solution.py:641
  144.6 1.4 copy.22
  146.1 2.0 %copy.23 = bf16[1,2880,128]{2,1,0:T(8,128)(2,1)} copy(bf16[1,2880,128]{2,1,0:T(8,128)(2,1)} %bitcast.10) | data formatting | bytes 1474560

commit v3 on v2

--- a/solution.py
+++ b/solution.py
@@ -15,7 +15,7 @@
 EPSILON = 1e-05
 CHUNKS = 4
 STRIDE = 11
-FIRST_BATCH = 12
+FIRST_BATCH = 6
 DOWN_EARLY = 16
 MESH = pl.DeviceIdType.MESH
 BF = jnp.bfloat16
@@ -44,7 +44,8 @@
 def kernel(
     n_expert,
     n_head,
-    pos_ref,
+    old_slot_ref,
+    new_slot_ref,
     new_ref,
     len_ref,
     sink_ref,
@@ -83,6 +84,8 @@
     ret_in,
     sync_in,
     sync_f,
+    logit_all,
+    route_all,
     sem,
     tok_sem,
     ag_sem,
@@ -162,13 +165,20 @@
     def drain(ref, s):
         pltpu.make_async_copy(ref, ref, s).wait()
 
+    def position(slot):
+        expert = new_slot_ref[slot]
+        found = jnp.int32(0)
+        for k in range(1, experts):
+            found = jnp.where(old_slot_ref[k] == expert, k, found)
+        return found
+
     def prepare_gate_up(slot):
-        index = pos_ref[slot]
+        index = position(slot)
         for c in range(2):
             gu_out[slot, :block, c * units : (c + 1) * units] = gate_up_ref[index, :, c, :]
 
     def prepare_down(slot):
-        index = pos_ref[slot]
+        index = position(slot)
         for p in range(2):
             dn_out[slot, :block, p * half : (p + 1) * half] = down_f[
                 p, pl.ds(index, block, stride=experts), :
@@ -296,14 +306,17 @@
     lax.fori_loop(1, FIRST_BATCH, send_gate_up, 0)
 
     new_col = column(new_ref[...].astype(F32), experts)
-    logits = [logit_ref[j : j + 1, :] for j in range(TOP)]
+    for s in range(STEPS):
+        logit_all[:, s * seqs : (s + 1) * seqs] = logit_ref[s]
+        route_all[:, s * seqs : (s + 1) * seqs] = route_ref[s].astype(F32)
+    logits = [logit_all[j : j + 1, :] for j in range(TOP)]
     highest = functools.reduce(jnp.maximum, logits)
     powers = [jnp.exp(l - highest) for l in logits]
     power_sum = functools.reduce(jnp.add, powers)
     member = jnp.zeros((experts, cols), F32)
     weight = jnp.zeros((experts, cols), F32)
     for j in range(TOP):
-        hit = (route_ref[j : j + 1, :].astype(F32) == new_col).astype(F32)
+        hit = (route_all[j : j + 1, :] == new_col).astype(F32)
         member += hit
         weight += hit * (powers[j] / power_sum)
     u0 = iota((cols, cols), 0)
@@ -346,7 +359,10 @@
     for b in range(1, per_head):
         gap += pad * (iota((share, wide), 0) >= b * block).astype(jnp.int32)
     stretch = (iota((share, wide), 0) + gap == lane).astype(BF)
-    gained = hidden * gain_ref[pl.ds(head, 1), :]
+    gain = jnp.zeros((1, share), F32)
+    for j in range(n_head):
+        gain += jnp.where(head == j, gain_ref[:, j * share : (j + 1) * share], 0.0)
+    gained = hidden * gain
     drain(square_in.at[pl.ds(0, n_head - 1)], sem.at[SQ_R])
     all_squares = jnp.zeros((1, cols), F32)
     for j in range(n_head):
@@ -432,7 +448,10 @@
     size = per * ROWS
     part_size = size // 2
     sent = [experts, DOWN_EARLY]
-    for k in range(CHUNKS):
+    lanes_out = pl.ds(pl.multiple_of((1 - my_side) * half, half), half)
+    lanes_own = pl.ds(pl.multiple_of(my_side * half, half), half)
+
+    def part_sums(k):
         acc = jnp.zeros((size, 2 * units), F32)
         for j in range(0, n_chip, 2):
             rows_in = jnp.concatenate(
@@ -453,8 +472,8 @@
             pair_sem.at[k, 0],
         )
         feed(sent, experts // CHUNKS, experts)
-    feed(sent, experts, experts)
-    for k in range(CHUNKS):
+
+    def activate(k):
         drain(half_in.at[k], pair_sem.at[k, 0])
         acc = half_f[k, my_side] + half_in[k].astype(F32)
         gate = jnp.minimum(acc[:, :units], 7.0)
@@ -463,10 +482,6 @@
         act_all[my_side, k] = active.astype(BF)
         view = act_all.at[my_side, k]
         send(view, view, partner, head, sem.at[ACT_S], pair_sem.at[k, 1])
-
-    drain(dn_in, sem.at[DN_R])
-    lanes_out = pl.ds(pl.multiple_of((1 - my_side) * half, half), half)
-    lanes_own = pl.ds(pl.multiple_of(my_side * half, half), half)
 
     def run(k):
         drain(act_all.at[1 - my_side, k], pair_sem.at[k, 1])
@@ -487,27 +502,57 @@
                 rs_sem.at[k, 0],
             )
 
+    ring = n_chip == 4
+    mid = per // 2
+    right, left = lax.rem(chip + 1, n_chip), lax.rem(chip + n_chip - 1, n_chip)
+
+    def rows_of(k, p):
+        return pl.ds(k * per + p * mid, mid)
+
+    def to_chip(src, dst, to, sem_in):
+        send(src, dst, me, 2 * to + core, sem.at[Z_S], sem_in)
+
     def add_cores(k):
         drain(y_in.at[:, chunk(k)], rs_sem.at[k, 0])
-        for d in range(n_chip):
+        for d in (2, 1, 3, 0) if ring else range(n_chip):
             to = lax.rem(chip + d, n_chip)
             z = y_out[to, chunk(k)].astype(F32) + y_in[to, chunk(k)].astype(F32)
             z_out[to, chunk(k)] = z.astype(BF)
-            if d > 0:
-                send(
-                    z_out.at[to, chunk(k)],
-                    z_in.at[d - 1, chunk(k)],
-                    me,
-                    2 * to + core,
-                    sem.at[Z_S],
-                    rs_sem.at[k, d],
-                )
+            if not ring:
+                if d > 0:
+                    to_chip(
+                        z_out.at[to, chunk(k)], z_in.at[d - 1, chunk(k)], to, rs_sem.at[k, d]
+                    )
+            elif d == 2:
+                for p, side in enumerate((right, left)):
+                    view = z_out.at[to, rows_of(k, p)]
+                    to_chip(view, z_in.at[2, rows_of(k, p)], side, rs_sem.at[k, 1 + p])
+            elif d > 0:
+                p = (3 - d) // 2
+                view = z_out.at[to, rows_of(k, p)]
+                to_chip(view, z_in.at[1 - p, rows_of(k, p)], to, rs_sem.at[k, 3 + p])
+
+    def pass_on(k):
+        if ring:
+            for p, to in enumerate((right, left)):
+                view = z_in.at[2, rows_of(k, p)]
+                drain(view, rs_sem.at[k, 1 + p])
+                z = z_out[to, rows_of(k, p)].astype(F32) + z_in[2, rows_of(k, p)].astype(F32)
+                z_out[to, rows_of(k, p)] = z.astype(BF)
+                view = z_out.at[to, rows_of(k, p)]
+                to_chip(view, z_in.at[p, rows_of(k, p)], to, rs_sem.at[k, 5 + p])
 
     def add_chips(k):
         total = z_out[chip, chunk(k)].astype(F32)
-        for d in range(1, n_chip):
-            drain(z_in.at[d - 1, chunk(k)], rs_sem.at[k, d])
-            total += z_in[d - 1, chunk(k)].astype(F32)
+        if ring:
+            for p in range(2):
+                drain(z_in.at[1 - p, rows_of(k, p)], rs_sem.at[k, 3 + p])
+                drain(z_in.at[p, rows_of(k, p)], rs_sem.at[k, 5 + p])
+            total += z_in[0, chunk(k)].astype(F32) + z_in[1, chunk(k)].astype(F32)
+        else:
+            for d in range(1, n_chip):
+                drain(z_in.at[d - 1, chunk(k)], rs_sem.at[k, d])
+                total += z_in[d - 1, chunk(k)].astype(F32)
         ret_out[chunk(k)] = total.astype(BF)
 
         def give_back(i, carry):
@@ -527,35 +572,34 @@
 
         lax.fori_loop(0, per, give_back, 0)
 
-    for k in range(CHUNKS):
-        run(k)
+    for stage in range(CHUNKS + 6):
+        if 0 <= stage - 2 < CHUNKS:
+            activate(stage - 2)
+        if stage < CHUNKS:
+            part_sums(stage)
+            if stage == CHUNKS - 1:
+                feed(sent, experts, experts)
+        if stage == 3:
+            drain(dn_in, sem.at[DN_R])
+        if 0 <= stage - 3 < CHUNKS:
+            run(stage - 3)
+        if stage == CHUNKS + 2:
+            send(
+                dn_in.at[:, :, lanes_out],
+                sync_in.at[my_side],
+                partner,
+                head,
+                sem.at[SYNC_S],
+                sem.at[SYNC_R],
+            )
 
         @pl.when(gathers)
         def _():
-            if k > 0:
-                add_cores(k - 1)
-            if k > 1:
-                add_chips(k - 2)
-
-    @pl.when(gathers)
-    def _():
-        add_cores(CHUNKS - 1)
-        add_chips(CHUNKS - 2)
-
-    send(
-        dn_in.at[:, :, lanes_out],
-        sync_in.at[my_side],
-        partner,
-        head,
-        sem.at[SYNC_S],
-        sem.at[SYNC_R],
-    )
+            for shift, what in ((4, add_cores), (5, pass_on), (6, add_chips)):
+                if 0 <= stage - shift < CHUNKS:
+                    what(stage - shift)
+
     sync_in[my_side] = dn_in[:, :, lanes_own]
-
-    @pl.when(gathers)
-    def _():
-        add_chips(CHUNKS - 1)
-
     drain(sync_in.at[1 - my_side], sem.at[SYNC_R])
     for i in range(n_expert):
         h, r = divmod(i, per_head)
@@ -631,12 +675,6 @@
     size = n_expert // CHUNKS * ROWS
     n_chip = n_head // 2
     width = norm_gain.shape[0]
-    counter = jnp.arange(experts, dtype=jnp.int32)
-    position = jnp.sum(
-        jnp.where(old_experts[None, :] == new_experts[:, None], counter[None, :], 0), axis=1
-    )
-    logits = jnp.transpose(route_logits, (2, 0, 1)).reshape(TOP, cols)
-    choices = jnp.transpose(routes, (2, 0, 1)).reshape(TOP, cols)
     vmem = pl.BlockSpec(memory_space=pltpu.VMEM)
     out, synced = pl.pallas_call(
         functools.partial(kernel, n_expert, n_head),
@@ -644,7 +682,7 @@
             jax.ShapeDtypeStruct((STEPS, seqs, share), BF),
             jax.ShapeDtypeStruct((width, half), BF),
         ),
-        in_specs=[pl.BlockSpec(memory_space=pltpu.SMEM)] + [vmem] * 13,
+        in_specs=[pl.BlockSpec(memory_space=pltpu.SMEM)] * 2 + [vmem] * 13,
         out_specs=(vmem, vmem),
         scratch_shapes=[
             pltpu.VMEM((2, block * experts, half), F32),
@@ -670,23 +708,26 @@
             pltpu.VMEM((experts, ROWS, wide), BF),
             pltpu.VMEM((2, experts, padded, half), BF),
             pltpu.VMEM((width, half), F32),
+            pltpu.VMEM((TOP, cols), F32),
+            pltpu.VMEM((TOP, cols), F32),
             pltpu.SemaphoreType.DMA((18,)),
             pltpu.SemaphoreType.DMA((CHUNKS,)),
             pltpu.SemaphoreType.DMA((CHUNKS, n_chip)),
             pltpu.SemaphoreType.DMA((CHUNKS, 2)),
-            pltpu.SemaphoreType.DMA((CHUNKS, n_chip)),
+            pltpu.SemaphoreType.DMA((CHUNKS, 7)),
         ],
         compiler_params=pltpu.CompilerParams(
             collective_id=0, has_side_effects=True, vmem_limit_bytes=56 << 20
         ),
     )(
-        position,
+        old_experts,
+        new_experts,
         new_experts.reshape(1, -1),
         cache_lengths.reshape(1, -1),
         sink_logits.reshape(1, -1),
-        logits,
-        choices,
-        norm_gain.reshape(n_head, share),
+        jnp.transpose(route_logits, (0, 2, 1)),
+        jnp.transpose(routes, (0, 2, 1)),
+        norm_gain.reshape(1, -1),
         queries,
         cache_band,
         new_kv,

time: 150 us -> 147 us (0.980)
  local copies, waits for them, and re-layouts: 7.55 us -> 4.76 us
  Pallas kernels: 139 us -> 141 us
    pallas_call x1, Pallas kernels: 139 us -> 141 us  [local(): pl.pallas_call(functools.partial(kernel, n_expert, n_head), out_shape=(ja...]
where the time goes in v3:
time: 147 us; the launch traced here: 146 us
  Pallas kernels  141 us (96%)
  local copies, waits for them, and re-layouts  4.76 us (3%)
    pallas_call x1, Pallas kernels, local(): pl.pallas_call(functools.partial(kernel, n_expert, n_head), out_shape=(ja...  141 us
    unnamed x2, local copies, waits for them, and re-layouts  3.45 us

profile of v3, /device:TPU:56, one launch (start us, length us, event | category | flops | bytes accessed | tf_op | source)
XLA Modules:
  0.0 146.3 jit_solution(2619263941958618357)
XLA Ops:
  0.6 1.3 reshape.19.gain_ref
  1.9 140.9 %shard_map.149 = (bf16[2,32,360]{2,1,0:T(8,128)(2,1)}, bf16[2880,128]{1,0:T(8,128)(2,1)}) custom-call(s32[32]{0:T(128)} %old_slot_ref.1, s32[32]{0:T(128)} %new_slot_ref.1, s32[1,32]{1,0:T(1,128)} %bitcast.13, s32[1,32]{1,0:T(1,128)} %bitcast.14, f32[1,4]{1,0:T(1,128)} %bitcast.15, f32[2,4,32]{2,1,0:T(4,128)} %bitcast.11, s32[2,4,32]{2,1,0:T(4,128)} %bitcast.12, ...), custom_call_target="tpu_custom_call" | custom-call | tf_op jit(solution)/shard_map/pallas_call | solution.py:679
  142.9 1.4 copy.18
  144.3 2.0 %copy.19 = bf16[1,2880,128]{2,1,0:T(8,128)(2,1)} copy(bf16[1,2880,128]{2,1,0:T(8,128)(2,1)} %bitcast.10) | data formatting | bytes 1474560

commit v4 on v3

--- a/solution.py
+++ b/solution.py
@@ -53,12 +53,12 @@
     route_ref,
     gain_ref,
     query_ref,
-    band_ref,
+    band_hbm,
     new_kv_ref,
-    o_ref,
+    o_hbm,
     residual_ref,
-    gate_up_ref,
-    down_ref,
+    gate_up_hbm,
+    down_hbm,
     out_ref,
     sync_ref,
     down_f,
@@ -86,6 +86,11 @@
     sync_f,
     logit_all,
     route_all,
+    band_ref,
+    o_ref,
+    gate_up_ref,
+    down_ref,
+    load_sem,
     sem,
     tok_sem,
     ag_sem,
@@ -123,6 +128,20 @@
     gathers = my_side == core
     keeps_rows = my_side == row_side
 
+    loads = [
+        pltpu.make_async_copy(a, b, load_sem.at[i])
+        for i, (a, b) in enumerate(
+            (
+                (down_hbm, down_ref),
+                (band_hbm, band_ref),
+                (o_hbm, o_ref),
+                (gate_up_hbm, gate_up_ref),
+            )
+        )
+    ]
+    for load in loads:
+        load.start()
+
     barrier = pltpu.get_barrier_semaphore()
 
     def greet_expert(i, carry):
@@ -140,6 +159,7 @@
     lax.fori_loop(1, n_expert, greet_expert, 0)
     lax.fori_loop(1, n_head, greet_head, 0)
 
+    loads[0].wait()
     for p in range(2):
         down_f[p] = (
             down_ref[:, :, p * half : (p + 1) * half].astype(F32).reshape(block * experts, half)
@@ -233,6 +253,7 @@
         jnp.where(row_g == iota((rows, GROUP), 1), sink_ref[...], 0.0), axis=1, keepdims=True
     )
     scale = HD**-0.5
+    loads[1].wait()
     batched = (((2,), (2,)), ((0,), (0,)))
     scores = (
         lax.dot_general(
@@ -273,9 +294,11 @@
         attended += dot((same_t & ((rt_id & 3) == g)).astype(BF), part)
     attended = attended.astype(BF)
 
+    loads[2].wait()
     for j in range(n_head):
         part_out[j] = dot(attended, o_ref[j * share : (j + 1) * share, :], ((1,), (1,))).astype(BF)
 
+    loads[3].wait()
     pl.semaphore_wait(barrier, n_expert + n_head - 2)
 
     def send_part(i, carry):
@@ -361,7 +384,7 @@
     stretch = (iota((share, wide), 0) + gap == lane).astype(BF)
     gain = jnp.zeros((1, share), F32)
     for j in range(n_head):
-        gain += jnp.where(head == j, gain_ref[:, j * share : (j + 1) * share], 0.0)
+        gain += jnp.where(head == j, gain_ref[j * share : (j + 1) * share].reshape(1, share), 0.0)
     gained = hidden * gain
     drain(square_in.at[pl.ds(0, n_head - 1)], sem.at[SQ_R])
     all_squares = jnp.zeros((1, cols), F32)
@@ -676,13 +699,16 @@
     n_chip = n_head // 2
     width = norm_gain.shape[0]
     vmem = pl.BlockSpec(memory_space=pltpu.VMEM)
+    hbm = pl.BlockSpec(memory_space=pl.ANY)
     out, synced = pl.pallas_call(
         functools.partial(kernel, n_expert, n_head),
         out_shape=(
             jax.ShapeDtypeStruct((STEPS, seqs, share), BF),
             jax.ShapeDtypeStruct((width, half), BF),
         ),
-        in_specs=[pl.BlockSpec(memory_space=pltpu.SMEM)] * 2 + [vmem] * 13,
+        in_specs=[pl.BlockSpec(memory_space=pltpu.SMEM)] * 2
+        + [vmem] * 7
+        + [hbm, vmem, hbm, vmem, hbm, hbm],
         out_specs=(vmem, vmem),
         scratch_shapes=[
             pltpu.VMEM((2, block * experts, half), F32),
@@ -710,6 +736,11 @@
             pltpu.VMEM((width, half), F32),
             pltpu.VMEM((TOP, cols), F32),
             pltpu.VMEM((TOP, cols), F32),
+            pltpu.VMEM(cache_band.shape, BF),
+            pltpu.VMEM(o_weight.shape[::-1], BF),
+            pltpu.VMEM(train_gate_up.shape, BF),
+            pltpu.VMEM((block, experts, units), BF),
+            pltpu.SemaphoreType.DMA((4,)),
             pltpu.SemaphoreType.DMA((18,)),
             pltpu.SemaphoreType.DMA((CHUNKS,)),
             pltpu.SemaphoreType.DMA((CHUNKS, n_chip)),
@@ -727,7 +758,7 @@
         sink_logits.reshape(1, -1),
         jnp.transpose(route_logits, (0, 2, 1)),
         jnp.transpose(routes, (0, 2, 1)),
-        norm_gain.reshape(1, -1),
+        norm_gain,
         queries,
         cache_band,
         new_kv,

time: 147 us -> 144 us (0.980); the launches traced: 146 us -> 141 us
  Pallas kernels: 141 us -> 137 us
    pallas_call x1, Pallas kernels: 141 us -> 137 us  [local(): pl.pallas_call(functools.partial(kernel, n_expert, n_head), out_shape=(ja...]
where the time goes in v4:
time: 144 us; the launch traced here: 141 us
  Pallas kernels  137 us (95%)
  local copies, waits for them, and re-layouts  3.45 us (2%)
    pallas_call x1, Pallas kernels, local(): pl.pallas_call(functools.partial(kernel, n_expert, n_head), out_shape=(ja...  137 us
    unnamed x2, local copies, waits for them, and re-layouts  3.45 us

profile of v4, /device:TPU:56, one launch (start us, length us, event | category | flops | bytes accessed | tf_op | source)
XLA Modules:
  0.0 140.9 jit_solution(16364741535071109111)
XLA Ops:
  0.6 136.8 %shard_map.149 = (bf16[2,32,360]{2,1,0:T(8,128)(2,1)}, bf16[2880,128]{1,0:T(8,128)(2,1)}) custom-call(s32[32]{0:T(128)} %old_slot_ref.1, s32[32]{0:T(128)} %new_slot_ref.1, s32[1,32]{1,0:T(1,128)} %bitcast.13, s32[1,32]{1,0:T(1,128)} %bitcast.14, f32[1,4]{1,0:T(1,128)} %bitcast.15, f32[2,4,32]{2,1,0:T(4,128)} %bitcast.11, s32[2,4,32]{2,1,0:T(4,128)} %bitcast.12, ...), custom_call_target="tpu_custom_call" | custom-call | tf_op jit(solution)/shard_map/pallas_call | solution.py:703
  137.5 1.4 %copy.18 = bf16[2,32,360]{2,1,0:T(8,128)(2,1)} copy(bf16[2,32,360]{2,1,0:T(8,128)(2,1)} %get-tuple-element.8) | data formatting | bytes 92160
  138.9 2.0 %copy.19 = bf16[1,2880,128]{2,1,0:T(8,128)(2,1)} copy(bf16[1,2880,128]{2,1,0:T(8,128)(2,1)} %bitcast.10) | data formatting | bytes 1474560

commit v5 on v4

--- a/solution.py
+++ b/solution.py
@@ -14,7 +14,7 @@
 ROWS = STEPS * CAP
 EPSILON = 1e-05
 CHUNKS = 4
-STRIDE = 11
+STRIDE = 9
 FIRST_BATCH = 6
 DOWN_EARLY = 16
 MESH = pl.DeviceIdType.MESH

time: 144 us -> 136 us (0.944); the launches traced: 141 us -> 135 us
  Pallas kernels: 137 us -> 131 us
    pallas_call x1, Pallas kernels: 137 us -> 131 us  [local(): pl.pallas_call(functools.partial(kernel, n_expert, n_head), out_shape=(ja...]
where the time goes in v5:
time: 136 us; the launch traced here: 135 us
  Pallas kernels  131 us (96%)
  local copies, waits for them, and re-layouts  3.45 us (3%)
    pallas_call x1, Pallas kernels, local(): pl.pallas_call(functools.partial(kernel, n_expert, n_head), out_shape=(ja...  131 us
    unnamed x2, local copies, waits for them, and re-layouts  3.45 us

profile of v5, /device:TPU:56, one launch (start us, length us, event | category | flops | bytes accessed | tf_op | source)
XLA Modules:
  0.0 135.4 jit_solution(2726431149674605992)
XLA Ops:
  0.6 131.3 %shard_map.149 = (bf16[2,32,360]{2,1,0:T(8,128)(2,1)}, bf16[2880,128]{1,0:T(8,128)(2,1)}) custom-call(s32[32]{0:T(128)} %old_slot_ref.1, s32[32]{0:T(128)} %new_slot_ref.1, s32[1,32]{1,0:T(1,128)} %bitcast.13, s32[1,32]{1,0:T(1,128)} %bitcast.14, f32[1,4]{1,0:T(1,128)} %bitcast.15, f32[2,4,32]{2,1,0:T(4,128)} %bitcast.11, s32[2,4,32]{2,1,0:T(4,128)} %bitcast.12, ...), custom_call_target="tpu_custom_call" | custom-call | tf_op jit(solution)/shard_map/pallas_call | solution.py:703
  132.0 1.4 %copy.18 = bf16[2,32,360]{2,1,0:T(8,128)(2,1)} copy(bf16[2,32,360]{2,1,0:T(8,128)(2,1)} %get-tuple-element.8) | data formatting | bytes 92160
  133.4 2.0 %copy.19 = bf16[1,2880,128]{2,1,0:T(8,128)(2,1)} copy(bf16[1,2880,128]{2,1,0:T(8,128)(2,1)} %bitcast.10) | data formatting | bytes 1474560
